TPU v7x, 128 devices: a whole 4x4x4 slice. The times are simulated.
128 devices in a mesh: pts: 32 (over x, y, core), mdl: 4 (over z).
Axes of the slice: x: 4, y: 4, z: 4, core: 2. Of those that a mesh axis runs over, the one named last changes fastest.
Arguments:
- points: bfloat16 [65536, 256], P(('pts', 'mdl')), may hold values from -6 to 6
- to_hilbert: int32 [65536], P(('pts', 'mdl')), may hold values from 0 to 65535, as said below
- parent: int32 [65536], P(('pts', 'mdl')), may hold values from 0 to 32767, as said below
- w_qkv: bfloat16 [256, 768], replicated
- w_out: bfloat16 [256, 256], replicated, may hold values from -0.375 to 0.375
- w_pool: bfloat16 [256, 512], replicated, may hold values from -0.375 to 0.375
- w_up: bfloat16 [512, 256], replicated, may hold values from -0.25 to 0.25
- w_skip: bfloat16 [256, 256], replicated, may hold values from -0.375 to 0.375
Outputs:
- pooled: bfloat16 [32768, 512], P(('pts', 'mdl'))
- decoded: bfloat16 [65536, 256], P(('pts', 'mdl'))
Inputs may be any that keep to these rules, and one draw needn't show every extreme that they name: `to_hilbert`: A permutation of the points. Of the 512 points of one device, at most 8 have Hilbert positions on any one device (positions are held 512 a device in order), and some pair of devices reaches 8. `parent`: never decreases along the points; every pooled index has at least one point. Pooled indices are held 256 a device in order; the points of a device belong to that device's pooled indices, except at most two leading points that belong to the last pooled index of the device before; some device has two such points.
All inputs are finite; a program needn't handle non-finite values.
Results may differ from a plain program's by a relative error of at most 0.02.
Values may be sent and summed in bfloat16 or wider, within the bound.
A program may use at most 64 MiB of HBM per device.

v0:
```python
import jax
import jax.numpy as jnp
from jax import lax
from jax.sharding import PartitionSpec as P

HEADS = 16
PATCH = 1024


epsilon = 1e-05


def passed_along(x, axis, by):
    devices = lax.axis_size(axis)
    pairs = [(i, i + by) for i in range(devices) if 0 <= i + by < devices]
    return lax.ppermute(x, axis, pairs)


def layer_norm(values):
    center = values - jnp.mean(values, axis=-1, keepdims=True)
    spread = jnp.mean(center * center, axis=-1, keepdims=True)
    return center * lax.rsqrt(spread + epsilon)


def on_device(points, to_hilbert, parent, w_qkv, w_out, w_pool, w_up, w_skip):
    row_count, channels = points.shape
    devices = lax.axis_size(("pts", "mdl"))
    group_count = lax.axis_size("mdl")
    capacity = 2 * row_count // devices
    local_heads = HEADS // group_count
    head_width = channels // HEADS
    group_width = channels // group_count
    score_scale = head_width ** (-0.5)
    target_dev = to_hilbert // row_count
    target_row = to_hilbert % row_count
    matches = (target_dev[:, None] == jnp.arange(devices, dtype=jnp.int32)[None, :]).astype(
        jnp.int32
    )
    earlier = jnp.cumsum(matches, axis=0) - matches
    slot_index = jnp.sum(earlier * matches, axis=1)
    bucket_pos = target_dev * capacity + slot_index
    outgoing = jnp.zeros((devices * capacity, channels), jnp.bfloat16).at[bucket_pos].set(points)
    targets = jnp.full((devices * capacity,), -1, jnp.int32).at[bucket_pos].set(target_row)
    arrived, arrived_pos = (
        lax.all_to_all(
            outgoing.reshape(devices, capacity, channels),
            ("pts", "mdl"),
            split_axis=0,
            concat_axis=0,
            tiled=True,
        ),
        lax.all_to_all(
            targets.reshape(devices, capacity),
            ("pts", "mdl"),
            split_axis=0,
            concat_axis=0,
            tiled=True,
        ),
    )
    arrived = arrived.reshape(devices * capacity, channels)
    arrived_pos = arrived_pos.reshape(devices * capacity)
    filled = arrived_pos >= 0
    placing = jnp.where(filled, arrived_pos, row_count)
    ordered = jnp.zeros((row_count, channels), jnp.bfloat16).at[placing].set(arrived, mode="drop")
    normed = layer_norm(ordered.astype(jnp.float32)).astype(jnp.bfloat16)
    arranged = (
        w_qkv.reshape(channels, 3, group_count, group_width)
        .transpose(0, 2, 1, 3)
        .reshape(channels, 3 * channels)
    )
    projected = jnp.dot(normed, arranged, preferred_element_type=jnp.float32).astype(jnp.bfloat16)
    projected = projected.reshape(row_count, group_count, 3 * group_width)
    gathered = lax.all_to_all(projected, "mdl", split_axis=1, concat_axis=0, tiled=True)
    patches = gathered.reshape(group_count * row_count // PATCH, PATCH, 3, local_heads, head_width)

    def attend(patch_block):
        scores = (
            jnp.einsum(
                "qhd,khd->hqk",
                patch_block[:, 0],
                patch_block[:, 1],
                preferred_element_type=jnp.float32,
            )
            * score_scale
        )
        highest = jnp.max(scores, axis=-1, keepdims=True)
        weights = jnp.exp(scores - highest)
        probs = (weights / jnp.sum(weights, axis=-1, keepdims=True)).astype(jnp.bfloat16)
        result = jnp.einsum(
            "hqk,khd->qhd", probs, patch_block[:, 2], preferred_element_type=jnp.float32
        )
        return result.astype(jnp.bfloat16).reshape(PATCH, group_width)

    attended = lax.map(attend, patches).reshape(group_count * row_count, group_width)
    head_rows = lax.dynamic_slice_in_dim(w_out, lax.axis_index("mdl") * group_width, group_width, 0)
    mixing = lax.psum_scatter(
        jnp.dot(attended, head_rows, preferred_element_type=jnp.float32).astype(jnp.bfloat16),
        "mdl",
        scatter_dimension=0,
        tiled=True,
    ).astype(jnp.float32)
    encoded_h = (ordered.astype(jnp.float32) + mixing).astype(jnp.bfloat16)
    sending = jnp.where(
        filled[:, None], encoded_h[jnp.where(filled, arrived_pos, 0)], jnp.zeros((), jnp.bfloat16)
    )
    returned = lax.all_to_all(
        sending.reshape(devices, capacity, channels),
        ("pts", "mdl"),
        split_axis=0,
        concat_axis=0,
        tiled=True,
    )
    encoded = returned.reshape(devices * capacity, channels)[bucket_pos]
    pooled_count = row_count // 2
    own_parent = parent - lax.axis_index(("pts", "mdl")) * pooled_count
    member = (own_parent[:, None] == jnp.arange(pooled_count, dtype=jnp.int32)[None, :]).astype(
        jnp.bfloat16
    )
    totals = jnp.einsum("rp,rc->pc", member, encoded, preferred_element_type=jnp.float32)
    tallies = jnp.sum(member.astype(jnp.float32), axis=0)
    spilled = (own_parent < 0).astype(jnp.float32)
    spill_sum = jnp.sum(spilled[:, None] * encoded.astype(jnp.float32), axis=0)[None, :]
    spill_tally = jnp.sum(spilled)[None]
    taken_sum, taken_tally = passed_along((spill_sum, spill_tally), ("pts", "mdl"), -1)
    totals = totals.at[pooled_count - 1].add(taken_sum[0])
    tallies = tallies.at[pooled_count - 1].add(taken_tally[0])
    pooled_in = (totals / tallies[:, None]).astype(jnp.bfloat16)
    pooled = jax.nn.gelu(
        layer_norm(jnp.dot(pooled_in, w_pool, preferred_element_type=jnp.float32))
    ).astype(jnp.bfloat16)
    lifted = jax.nn.gelu(
        layer_norm(jnp.dot(pooled, w_up, preferred_element_type=jnp.float32))
    ).astype(jnp.bfloat16)
    carried = passed_along(lifted[pooled_count - 1 :], ("pts", "mdl"), 1)
    picked = jnp.dot(member, lifted, preferred_element_type=jnp.float32) + spilled[
        :, None
    ] * carried.astype(jnp.float32)
    skipped = jax.nn.gelu(layer_norm(jnp.dot(encoded, w_skip, preferred_element_type=jnp.float32)))
    decoded = (skipped + picked).astype(jnp.bfloat16)
    return (pooled, decoded)


def solution(mesh):
    in_specs = (
        P(("pts", "mdl"), None),
        P(("pts", "mdl")),
        P(("pts", "mdl")),
        P(),
        P(),
        P(),
        P(),
        P(),
    )
    out_specs = (P(("pts", "mdl"), None), P(("pts", "mdl"), None))
    return jax.shard_map(
        on_device, mesh=mesh, in_specs=in_specs, out_specs=out_specs, check_vma=False
    )
```

profile of v0, /device:TPU:1, one launch (start us, length us, event | category | flops | bytes accessed | tf_op | source)
XLA Modules:
  0.0 219.4 jit_solution(9377016021376559816)
XLA Ops:
  8.6 2.4 %scatter_custom_fusion = s32[1024]{0:T(1024)S(1)} fusion(s32[512]{0:T(512)S(1)} %compare_select_fusion.4, s32[512]{0:T(512)S(1)} %get-tuple-element.76, s32[]{:T(128)} %constant.142.clone.1), kind=kCustom, calls=%fused_computation.109 | custom fusion | bytes 4100 | tf_op jit(solution)/shard_map/scatter | solution.py:43
  11.8 11.5 %all-to-all-start = ((s32[128,1,8]{2,1,0:T(1,128)}), s32[128,1,8]{2,1,0:T(1,128)S(1)}, u32[]{:S(2)}, u32[]{:S(2)}) async-start(s32[128,1,8]{2,1,0:T(1,128)} %bitcast.10), calls=%async_computation | async-start | bytes 131072 | tf_op jit(solution)/shard_map/all_to_all | solution.py:52
  23.3 3.5 %scatter_custom_fusion.1 = bf16[1024,256]{1,0:T(8,128)(2,1)} fusion(s32[512]{0:T(512)S(1)} %compare_select_fusion.4, bf16[512,256]{1,0:T(8,128)(2,1)} %param.14, bf16[]{:T(256)} %constant.150.clone.1), kind=kCustom, calls=%fused_computation.78 | custom fusion | bytes 524800 | tf_op jit(solution)/shard_map/scatter | solution.py:42
  26.8 6.1 %all-to-all-done = s32[128,1,8]{2,1,0:T(1,128)S(1)} async-done(((s32[128,1,8]{2,1,0:T(1,128)}), s32[128,1,8]{2,1,0:T(1,128)S(1)}, u32[]{:S(2)}, u32[]{:S(2)}) %all-to-all-start) | async-done | bytes 4128 | tf_op jit(solution)/shard_map/all_to_all | solution.py:52
  32.9 4.3 %all-to-all-start.1 = ((bf16[128,8,256]{2,1,0:T(8,128)(2,1)}), bf16[128,8,256]{2,1,0:T(8,128)(2,1)S(1)}, u32[]{:S(2)}, u32[]{:S(2)}) async-start(bf16[128,8,256]{2,1,0:T(8,128)(2,1)} %bitcast.13), calls=%async_computation.1 | async-start | bytes 1048576 | tf_op jit(solution)/shard_map/all_to_all | solution.py:45
  37.2 1.2 copy.60
  40.4 10.7 %all-to-all-done.1 = bf16[128,8,256]{2,1,0:T(8,128)(2,1)S(1)} async-done(((bf16[128,8,256]{2,1,0:T(8,128)(2,1)}), bf16[128,8,256]{2,1,0:T(8,128)(2,1)S(1)}, u32[]{:S(2)}, u32[]{:S(2)}) %all-to-all-start.1) | async-done | bytes 524320 | tf_op jit(solution)/shard_map/all_to_all | solution.py:45
  51.1 5.0 %scatter_custom_fusion.2 = bf16[512,256]{1,0:T(8,128)(2,1)S(1)} fusion(s32[1024]{0:T(1024)S(1)} %bitcast.89, bf16[128,8,256]{2,1,0:T(8,128)(2,1)S(1)} %all-to-all-done.1, bf16[]{:T(256)} %constant.150.clone.1), kind=kCustom, calls=%fused_computation.52 | custom fusion | bytes 786434 | tf_op jit(solution)/shard_map/scatter | solution.py:64
  57.0 1.2 copy.62
  58.2 3.5 %all-to-all-start.2 = ((bf16[512,4,192]{0,2,1:T(8,128)(2,1)}), bf16[512,4,192]{0,2,1:T(8,128)(2,1)S(1)}, u32[]{:S(2)}, u32[]{:S(2)}) async-start(bf16[512,4,192]{0,2,1:T(8,128)(2,1)} %bitcast.18), calls=%async_computation.2 | async-start | bytes 1572864 | tf_op jit(solution)/shard_map/all_to_all | solution.py:73
  61.9 11.7 %all-to-all-done.2 = bf16[512,4,192]{0,2,1:T(8,128)(2,1)S(1)} async-done(((bf16[512,4,192]{0,2,1:T(8,128)(2,1)}), bf16[512,4,192]{0,2,1:T(8,128)(2,1)S(1)}, u32[]{:S(2)}, u32[]{:S(2)}) %all-to-all-start.2) | async-done | bytes 786464 | tf_op jit(solution)/shard_map/all_to_all | solution.py:73
  75.0 71.4 %while.12 = (s32[]{:T(128)}, bf16[2,1024,64]{1,2,0:T(8,128)(2,1)S(1)}, bf16[2,1024,3,4,16]{1,4,3,2,0:T(8,128)(2,1)S(1)}, s32[]{:T(128)}) while((s32[]{:T(128)}, bf16[2,1024,64]{1,2,0:T(8,128)(2,1)S(1)}, bf16[2,1024,3,4,16]{1,4,3,2,0:T(8,128)(2,1)S(1)}, s32[]{:T(128)}) %tuple.45), condition=%wide.region_11.12_spmd, body=%wide.region_8.11_spmd.sunk | while | flops 306255872 | bytes 68714568 | solution.py:94
  75.1 8.1 %fusion.90 = f32[4,1024,1024]{1,2,0:T(8,128)} fusion(bf16[1024,3,4,16]{0,3,2,1:T(8,128)(2,1)S(1)} %dynamic-slice_bitcast_fusion.2), kind=kOutput, calls=%fused_computation.15.clone.1 | convolution fusion | flops 134217728 | bytes 17039360 | tf_op jit(solution)/shard_map/while/body/eval_jaxpr/qhd,khd->hqk/dot_general | solution.py:78
  83.2 12.6 %fusion.91 = f32[4,1024]{1,0:T(4,128)S(1)} fusion(f32[4,1024,1024]{1,2,0:T(8,128)} %fusion.90), kind=kOutput, calls=%fused_computation.125.clone.1 | output fusion | flops 16778240 | bytes 16793600 | tf_op jit(solution)/shard_map/while/body/eval_jaxpr/sub | solution.py:87
  95.7 14.9 %fusion.92 = bf16[4,16,1024]{2,1,0:T(8,128)(2,1)S(1)} fusion(f32[4,1024]{1,0:T(4,128)S(1)} %fusion.91, bf16[1024,3,4,16]{0,3,2,1:T(8,128)(2,1)S(1)} %dynamic-slice_bitcast_fusion.2, f32[4,1024,1024]{1,2,0:T(8,128)} %fusion.90), kind=kOutput, calls=%fused_computation.12.clone.1 | convolution fusion | flops 155259904 | bytes 33832960 | tf_op jit(solution)/shard_map/while/body/eval_jaxpr/hqk,khd->qhd/dot_general | solution.py:89
  110.8 8.1 %fusion.90 = f32[4,1024,1024]{1,2,0:T(8,128)} fusion(bf16[1024,3,4,16]{0,3,2,1:T(8,128)(2,1)S(1)} %dynamic-slice_bitcast_fusion.2), kind=kOutput, calls=%fused_computation.15.clone.1 | convolution fusion | flops 134217728 | bytes 17039360 | tf_op jit(solution)/shard_map/while/body/eval_jaxpr/qhd,khd->hqk/dot_general | solution.py:78
  118.8 12.6 %fusion.91 = f32[4,1024]{1,0:T(4,128)S(1)} fusion(f32[4,1024,1024]{1,2,0:T(8,128)} %fusion.90), kind=kOutput, calls=%fused_computation.125.clone.1 | output fusion | flops 16778240 | bytes 16793600 | tf_op jit(solution)/shard_map/while/body/eval_jaxpr/sub | solution.py:87
  131.4 14.9 %fusion.92 = bf16[4,16,1024]{2,1,0:T(8,128)(2,1)S(1)} fusion(f32[4,1024]{1,0:T(4,128)S(1)} %fusion.91, bf16[1024,3,4,16]{0,3,2,1:T(8,128)(2,1)S(1)} %dynamic-slice_bitcast_fusion.2, f32[4,1024,1024]{1,2,0:T(8,128)} %fusion.90), kind=kOutput, calls=%fused_computation.12.clone.1 | convolution fusion | flops 155259904 | bytes 33832960 | tf_op jit(solution)/shard_map/while/body/eval_jaxpr/hqk,khd->qhd/dot_general | solution.py:89
  146.4 2.3 %convolution_convert_fusion = bf16[2048,256]{1,0:T(8,128)(2,1)} fusion(bf16[2048,64]{0,1:T(8,128)(2,1)S(1)} %bitcast.83, bf16[256,256]{1,0:T(8,128)(2,1)} %param.18, s32[]{:T(128)S(6)} %select_n.71), kind=kOutput, calls=%fused_computation.22 | convolution fusion | flops 67633152 | bytes 1343492 | tf_op jit(solution)/shard_map/dot_general | solution.py:97
  149.4 3.9 %collective-permute-start.1 = (f32[1]{0:T(128)}, f32[1]{0:T(128)}, u32[]{:S(2)}, u32[]{:S(2)}) collective-permute-start(f32[1]{0:T(128)} %bitcast.25), channel_id=1, source_target_pairs={{1,0},{2,1},{3,2},{4,3},{5,4},{6,5},{7,6},{8,7},{9,8},{10,9},{11,1... | collective-permute-start | bytes 20 | tf_op jit(solution)/shard_map/ppermute | solution.py:16
  153.5 13.3 %reduce-scatter.2.cloned.1.call-done = bf16[512,256]{1,0:T(8,128)(2,1)} async-done(((bf16[2048,256]{1,0:T(8,128)(2,1)}), bf16[512,256]{1,0:T(8,128)(2,1)}) %reduce-scatter.2.cloned.1.call-update) | async-done | bytes 262160 | tf_op jit(solution)/shard_map/reduce_scatter | solution.py:96
  166.8 1.1 fusion.20
  167.9 3.9 %gather_fusion = bf16[1024,256]{1,0:T(8,128)(2,1)S(1)} fusion(bf16[512,256]{1,0:T(8,128)(2,1)S(1)} %fusion.20, s32[1024]{0:T(1024)S(1)} %broadcast_clamp_fusion), kind=kCustom, calls=%fused_computation | custom fusion | bytes 1052672 | tf_op jit(solution)/shard_map/gather | solution.py:104
  171.9 1.0 bitcast_select_fusion
  172.8 9.6 %all-to-all-start.3 = ((bf16[128,8,256]{2,1,0:T(8,128)(2,1)}), bf16[128,8,256]{2,1,0:T(8,128)(2,1)S(1)}, u32[]{:S(2)}, u32[]{:S(2)}) async-start(bf16[128,8,256]{2,1,0:T(8,128)(2,1)} %bitcast_select_fusion), calls=%async_computation.4 | async-start | bytes 1048576 | tf_op jit(solution)/shard_map/all_to_all | solution.py:106
  183.4 13.0 %all-to-all-done.3 = bf16[128,8,256]{2,1,0:T(8,128)(2,1)S(1)} async-done(((bf16[128,8,256]{2,1,0:T(8,128)(2,1)}), bf16[128,8,256]{2,1,0:T(8,128)(2,1)S(1)}, u32[]{:S(2)}, u32[]{:S(2)}) %all-to-all-start.3) | async-done | bytes 524320 | tf_op jit(solution)/shard_map/all_to_all | solution.py:106
  196.5 1.9 gather_fusion.1
  199.1 3.1 %collective-permute-start = (f32[1,256]{1,0:T(1,128)S(1)}, f32[1,256]{1,0:T(1,128)S(1)}, u32[]{:S(2)}, u32[]{:S(2)}) collective-permute-start(f32[1,256]{1,0:T(1,128)S(1)} %bitcast.90), channel_id=1, source_target_pairs={{1,0},{2,1},{3,2},{4,3},{5,4},{6,5},{7,6},{8,7},{9,8},{10,9},{11,1... | collective-permute-start | bytes 3080 | tf_op jit(solution)/shard_map/ppermute | solution.py:16
  202.6 0.8 collective-permute-done
  205.1 2.5 %collective-permute-start.2 = (bf16[1,256]{1,0:T(2,128)(2,1)S(1)}, bf16[1,256]{1,0:T(2,128)(2,1)S(1)}, u32[]{:S(2)}, u32[]{:S(2)}) collective-permute-start(bf16[1,256]{1,0:T(2,128)(2,1)S(1)} %slice.61), channel_id=1, source_target_pairs={{0,1},{1,2},{2,3},{3,4},{4,5},{5,6},{6,7},{7,8},{8,9},{9,10},{10,1... | collective-permute-start | bytes 1544 | tf_op jit(solution)/shard_map/ppermute | solution.py:16
  207.6 3.6 %collective-permute-done.2 = bf16[1,256]{1,0:T(2,128)(2,1)S(1)} collective-permute-done((bf16[1,256]{1,0:T(2,128)(2,1)S(1)}, bf16[1,256]{1,0:T(2,128)(2,1)S(1)}, u32[]{:S(2)}, u32[]{:S(2)}) %collective-permute-start.2) | collective-permute-done | bytes 544 | tf_op jit(solution)/shard_map/ppermute | solution.py:16
  211.7 0.8 copy.68
  (87 shorter events, 11.7 us)
Async XLA Ops:
  7.2 196.3 %copy-start = (bf16[256,512]{1,0:T(8,128)(2,1)S(1)}, bf16[256,512]{1,0:T(8,128)(2,1)}, u32[]{:S(2)}) copy-start(bf16[256,512]{1,0:T(8,128)(2,1)} %param.19) | copy-start | bytes 786436
  8.6 29.8 %copy-start.8 = (s32[512]{0:T(512)}, s32[512]{0:T(512)S(1)}, u32[]{:S(2)}) copy-start(s32[512]{0:T(512)S(1)} %compare_select_fusion.4) | copy-start | bytes 6148
  11.8 21.1 %all-to-all-start = ((s32[128,1,8]{2,1,0:T(1,128)}), s32[128,1,8]{2,1,0:T(1,128)S(1)}, u32[]{:S(2)}, u32[]{:S(2)}) async-start(s32[128,1,8]{2,1,0:T(1,128)} %bitcast.10), calls=%async_computation | async-start | bytes 131072 | tf_op jit(solution)/shard_map/all_to_all | solution.py:52
  32.9 18.2 %copy-start.3 = (s32[128,1,8]{2,1,0:T(1,128)}, s32[128,1,8]{2,1,0:T(1,128)S(1)}, u32[]{:S(2)}) copy-start(s32[128,1,8]{2,1,0:T(1,128)S(1)} %all-to-all-done) | copy-start | bytes 12292
  32.9 18.2 %all-to-all-start.1 = ((bf16[128,8,256]{2,1,0:T(8,128)(2,1)}), bf16[128,8,256]{2,1,0:T(8,128)(2,1)S(1)}, u32[]{:S(2)}, u32[]{:S(2)}) async-start(bf16[128,8,256]{2,1,0:T(8,128)(2,1)} %bitcast.13), calls=%async_computation.1 | async-start | bytes 1048576 | tf_op jit(solution)/shard_map/all_to_all | solution.py:45
  56.1 18.9 %copy-start.1 = (bf16[512,256]{1,0:T(8,128)(2,1)}, bf16[512,256]{1,0:T(8,128)(2,1)S(1)}, u32[]{:S(2)}) copy-start(bf16[512,256]{1,0:T(8,128)(2,1)S(1)} %scatter_custom_fusion.2) | copy-start | bytes 786436
  58.2 15.5 %all-to-all-start.2 = ((bf16[512,4,192]{0,2,1:T(8,128)(2,1)}), bf16[512,4,192]{0,2,1:T(8,128)(2,1)S(1)}, u32[]{:S(2)}, u32[]{:S(2)}) async-start(bf16[512,4,192]{0,2,1:T(8,128)(2,1)} %bitcast.18), calls=%async_computation.2 | async-start | bytes 1572864 | tf_op jit(solution)/shard_map/all_to_all | solution.py:73
  61.7 105.1 %reduce-scatter.2.cloned.1.call-start = ((), (), s32[]{:S(2)}) async-start(), calls=%async_computation.5 | async-start | bytes 1310720 | tf_op jit(solution)/shard_map/reduce_scatter | solution.py:96
  74.9 73.8 %copy-start.10 = (s32[512]{0:T(512)S(1)}, s32[512]{0:T(512)}, u32[]{:S(2)}) copy-start(s32[512]{0:T(512)} %param.16) | copy-start | bytes 6148
  75.0 78.3 %copy-start.4 = (s32[128,1,8]{2,1,0:T(1,128)S(1)}, s32[128,1,8]{2,1,0:T(1,128)}, u32[]{:S(2)}) copy-start(s32[128,1,8]{2,1,0:T(1,128)} %copy-done.3) | copy-start | bytes 12292
  75.0 78.5 %copy-start.7 = (s32[1024,1]{0,1:T(1,128)S(1)}, s32[1024,1]{0,1:T(1,128)}, u32[]{:S(2)}) copy-start(s32[1024,1]{0,1:T(1,128)} %get-tuple-element.74) | copy-start | bytes 12292
  75.0 107.5 %copy-start.9 = (s32[512]{0:T(512)S(1)}, s32[512]{0:T(512)}, u32[]{:S(2)}) copy-start(s32[512]{0:T(512)} %copy-done.8) | copy-start | bytes 6148
  75.0 127.2 %copy-start.6 = (bf16[256,256]{1,0:T(8,128)(2,1)S(1)}, bf16[256,256]{1,0:T(8,128)(2,1)}, u32[]{:S(2)}) copy-start(bf16[256,256]{1,0:T(8,128)(2,1)} %param.21) | copy-start | bytes 393220
  146.4 58.0 %copy-start.5 = (bf16[512,256]{1,0:T(8,128)(2,1)S(1)}, bf16[512,256]{1,0:T(8,128)(2,1)}, u32[]{:S(2)}) copy-start(bf16[512,256]{1,0:T(8,128)(2,1)} %param.20) | copy-start | bytes 786436
  149.4 33.3 %collective-permute-start.1 = (f32[1]{0:T(128)}, f32[1]{0:T(128)}, u32[]{:S(2)}, u32[]{:S(2)}) collective-permute-start(f32[1]{0:T(128)} %bitcast.25), channel_id=1, source_target_pairs={{1,0},{2,1},{3,2},{4,3},{5,4},{6,5},{7,6},{8,7},{9,8},{10,9},{11,1... | collective-permute-start | bytes 20 | tf_op jit(solution)/shard_map/ppermute | solution.py:16
  172.8 23.6 %all-to-all-start.3 = ((bf16[128,8,256]{2,1,0:T(8,128)(2,1)}), bf16[128,8,256]{2,1,0:T(8,128)(2,1)S(1)}, u32[]{:S(2)}, u32[]{:S(2)}) async-start(bf16[128,8,256]{2,1,0:T(8,128)(2,1)} %bitcast_select_fusion), calls=%async_computation.4 | async-start | bytes 1048576 | tf_op jit(solution)/shard_map/all_to_all | solution.py:106
  199.1 4.3 %collective-permute-start = (f32[1,256]{1,0:T(1,128)S(1)}, f32[1,256]{1,0:T(1,128)S(1)}, u32[]{:S(2)}, u32[]{:S(2)}) collective-permute-start(f32[1,256]{1,0:T(1,128)S(1)} %bitcast.90), channel_id=1, source_target_pairs={{1,0},{2,1},{3,2},{4,3},{5,4},{6,5},{7,6},{8,7},{9,8},{10,9},{11,1... | collective-permute-start | bytes 3080 | tf_op jit(solution)/shard_map/ppermute | solution.py:16
  204.4 8.2 %copy-start.2 = (bf16[256,512]{1,0:T(8,128)(2,1)}, bf16[256,512]{1,0:T(8,128)(2,1)S(1)}, u32[]{:S(2)}) copy-start(bf16[256,512]{1,0:T(8,128)(2,1)S(1)} %fusion.28) | copy-start | bytes 786436
  205.1 6.1 %collective-permute-start.2 = (bf16[1,256]{1,0:T(2,128)(2,1)S(1)}, bf16[1,256]{1,0:T(2,128)(2,1)S(1)}, u32[]{:S(2)}, u32[]{:S(2)}) collective-permute-start(bf16[1,256]{1,0:T(2,128)(2,1)S(1)} %slice.61), channel_id=1, source_target_pairs={{0,1},{1,2},{2,3},{3,4},{4,5},{5,6},{6,7},{7,8},{8,9},{9,10},{10,1... | collective-permute-start | bytes 1544 | tf_op jit(solution)/shard_map/ppermute | solution.py:16
Sparse Core Ops, SparseCore 0:
  148.8 17.9 reduce-scatter.1
where the time goes:
time: 222 us; the launch traced here: 219 us
  waiting for transfers between devices  59.3 us (27%)
  matrix products  50.6 us (23%)
  starting transfers between devices  38.5 us (17%)
  other arithmetic  33 us (15%)
  local copies, waits for them, and re-layouts  23.3 us (10%)
  between operations  14.5 us (7%)
    dot_general x2, matrix products, attend(): jnp.einsum('hqk,khd->qhd', probs, patch_block[:, 2], preferred_element_ty...  29.9 us
    sub x2, other arithmetic, attend(): weights = jnp.exp(scores - highest)  25.2 us
    dot_general x2, matrix products, attend(): jnp.einsum('qhd,khd->hqk', patch_block[:, 0], patch_block[:, 1], preferre...  16.2 us
    reduce_scatter x1, waiting for transfers between devices, on_device(): lax.psum_scatter(jnp.dot(attended, head_rows, preferred_element_type=jnp....  13.3 us
    all_to_all x1, waiting for transfers between devices, on_device(): lax.all_to_all(sending.reshape(devices, capacity, channels), ('pts', 'mdl...  13 us
    all_to_all x1, waiting for transfers between devices, on_device(): lax.all_to_all(projected, 'mdl', split_axis=1, concat_axis=0, tiled=True)  11.7 us
    all_to_all x1, starting transfers between devices, on_device(): lax.all_to_all(targets.reshape(devices, capacity), ('pts', 'mdl'), split_...  11.5 us
    all_to_all x1, waiting for transfers between devices, on_device(): lax.all_to_all(outgoing.reshape(devices, capacity, channels), ('pts', 'md...  10.7 us
  transfers between devices with their start and end apart: 8, of which 7 were waited for; matrix products, arithmetic and copies ran while one was open for 7% of the time, Pallas kernels for 0%

commit v1 on v0

v1 whole, which is shorter than its diff:
```python
import functools

import jax
import jax.numpy as jnp
from jax import lax
from jax.experimental import pallas as pl
from jax.experimental.pallas import tpu as pltpu
from jax.sharding import PartitionSpec as P

ROWS = 512
C = 256
C2 = 512
HEADS = 16
WIDTH = C // HEADS
POOL = ROWS // 2
DEVS = 128
CAP = 8
SLOTS = DEVS * CAP
BLK = 2 * CAP
EXT = POOL + 16
EMPTY = 64.0
QSCALE = WIDTH**-0.5 * 1.4426950408889634
MESH = pl.DeviceIdType.MESH
f32, bf16, i32 = jnp.float32, jnp.bfloat16, jnp.int32


def _offsets():
    far = lambda d: min(d, 4 - d)
    every = [(x, y, c, z) for x in range(4) for y in range(4) for z in range(4) for c in range(2)]
    every.sort(key=lambda o: -(far(o[0]) + far(o[1]) + far(o[3]) + 0.1 * o[2]))
    return [o for o in every if any(o)]


OFFSETS = _offsets()


def dot(a, b):
    return jnp.dot(a, b, preferred_element_type=f32)


def dot_nt(a, b):
    return lax.dot_general(a, b, (((1,), (1,)), ((), ())), preferred_element_type=f32)


def dot_tn(a, b):
    return lax.dot_general(a, b, (((0,), (0,)), ((), ())), preferred_element_type=f32)


def iota(shape, dim):
    return lax.broadcasted_iota(i32, shape, dim)


def onehot(cond):
    return jnp.where(cond, 1.0, 0.0).astype(bf16)


def layer_norm(v):
    center = v - jnp.mean(v, axis=-1, keepdims=True)
    spread = jnp.mean(center * center, axis=-1, keepdims=True)
    return center * lax.rsqrt(spread + 1e-5)


def gelu(v):
    return 0.5 * v * (1.0 + jnp.tanh(0.7978845608028654 * (v + 0.044715 * (v * v * v))))


def to_blocks(v):
    v = v.reshape(DEVS, CAP, C)
    return jnp.concatenate([v[:, :, :128], v[:, :, 128:]], axis=1).reshape(DEVS * BLK, 128)


def from_blocks(b):
    v = b.astype(f32).reshape(DEVS, BLK, 128)
    return jnp.concatenate([v[:, :CAP], v[:, CAP:]], axis=2).reshape(SLOTS, C)


def kernel(
    pt_ref, th_ref, par_ref, wqkv_ref, wout_ref, wpool_ref, wup_ref, wskip_ref,
    pooled_ref, dec_ref,
    out1, in1, out2, in2, bkt_t, comp_t, wq_t, wv_t, nrm, qtm, vta, keys, s_a, s_b, att, tot, tal, e_out, e_in,
    send1, recv1, loc1, send2, recv2, loc2, psend, precv, esend, erecv,
):
    pts, mdl = lax.axis_index("pts"), lax.axis_index("mdl")
    me = pts * 4 + mdl
    core, yy, xx = pts % 2, (pts // 2) % 4, pts // 8
    at_x = [((xx + d) % 4) * 8 for d in range(4)]
    at_y = [((yy + d) % 4) * 2 for d in range(4)]
    at_c = [(core + d) % 2 for d in range(2)]
    at_z = [(mdl + d) % 4 for d in range(4)]

    def place(o):
        return at_x[o[0]] + at_y[o[1]] + at_c[o[2]], at_z[o[3]]

    def block(line):
        return pl.ds(pl.multiple_of(line * BLK, BLK), BLK)

    barrier = pltpu.get_barrier_semaphore()
    for o in OFFSETS:
        pl.semaphore_signal(barrier, inc=1, device_id=place(o), device_id_type=MESH)

    half = th_ref[...] >> 9
    target = (half >> 3) * 8 + (half & 1) * 4 + ((half >> 1) & 3)
    match = jnp.where(iota((DEVS, ROWS), 0) == target, 1.0, 0.0)
    upper = onehot(iota((ROWS, ROWS), 0) < iota((ROWS, ROWS), 1))
    earlier = dot(match.astype(bf16), upper)
    rank = jnp.sum(match * earlier, axis=0, keepdims=True)
    slot = target * CAP + rank.astype(i32)
    bucket = jnp.where(iota((SLOTS, ROWS), 0) == slot, 1.0, 0.0)
    taken = jnp.sum(bucket, axis=1, keepdims=True)
    filled = dot(bucket.astype(bf16), pt_ref[...])
    lane = iota((1, C), 1)
    filled = filled + jnp.where(lane < 128, (1.0 - taken) * EMPTY, 0.0)
    out1[...] = to_blocks(filled).astype(bf16)

    pl.semaphore_wait(barrier, DEVS - 1)

    def exchange(src, dst, send, recv, loc):
        own = pltpu.make_async_copy(src.at[block(me)], dst.at[block(me)], loc)
        for o in OFFSETS:
            p, m = place(o)
            pltpu.make_async_remote_copy(
                src_ref=src.at[block(p * 4 + m)],
                dst_ref=dst.at[block(me)],
                send_sem=send,
                recv_sem=recv,
                device_id=(p, m),
                device_id_type=MESH,
            ).start()
        own.start()

    def finish(src, dst, send, recv, loc):
        most = pl.ds(0, (DEVS - 1) * BLK)
        pltpu.make_async_copy(src.at[block(0)], dst.at[block(0)], loc).wait()
        pltpu.make_async_copy(src.at[most], src.at[most], send).wait()
        pltpu.make_async_copy(dst.at[most], dst.at[most], recv).wait()

    exchange(out1, in1, send1, recv1, loc1)

    slot_cols = jnp.transpose(jnp.broadcast_to(slot.astype(f32), (128, ROWS)))
    lanes = iota((1, 128), 1).astype(f32)
    for k in range(SLOTS // 128):
        bkt_t[:, k * 128 : (k + 1) * 128] = onehot(slot_cols == lanes + k * 128.0)
    wq_t[...] = jnp.transpose(wqkv_ref[:, :C])
    wv_t[...] = jnp.transpose(wqkv_ref[:, 2 * C :])
    qtm[...] = jnp.zeros_like(qtm)
    for h in range(HEADS):
        vta[32 * h + 16 : 32 * h + 32] = jnp.ones((16, 2 * ROWS), bf16)
    lower = onehot(iota((SLOTS, SLOTS), 1) < iota((SLOTS, SLOTS), 0))

    finish(out1, in1, send1, recv1, loc1)

    arrived = from_blocks(in1[...])
    valid = jnp.broadcast_to(jnp.where(arrived[:, :1] < 32.0, 1.0, 0.0), (SLOTS, 128))
    place_of = jnp.where(valid > 0.0, dot(lower, valid.astype(bf16)), -1.0)
    for k in range(ROWS // 128):
        comp_t[:, k * 128 : (k + 1) * 128] = onehot(place_of == lanes + k * 128.0)
    place_row = jnp.transpose(place_of)[:1].astype(i32)
    comp = onehot(iota((ROWS, SLOTS), 0) == place_row)
    ordered = dot(comp, arrived.astype(bf16))
    normed = layer_norm(ordered).astype(bf16)
    nrm[0] = normed

    swap = pltpu.make_async_remote_copy(
        src_ref=nrm.at[0], dst_ref=nrm.at[1], send_sem=psend, recv_sem=precv,
        device_id=(at_x[0] + at_y[0] + at_c[1], mdl), device_id_type=MESH,
    )
    swap.start()

    queries = (dot_nt(wq_t[...], normed) * QSCALE).astype(bf16)
    for h in range(HEADS):
        low = h * 128 + (16 * h) % 128
        qtm[low : low + 16] = queries[16 * h : 16 * h + 16]

    def project(part, rows):
        keys[part * ROWS : (part + 1) * ROWS] = dot(rows, wqkv_ref[:, C : 2 * C]).astype(bf16)
        values = dot_nt(wv_t[...], rows).astype(bf16)
        for h in range(HEADS):
            vta[32 * h : 32 * h + 16, part * ROWS : (part + 1) * ROWS] = values[16 * h : 16 * h + 16]

    project(0, normed)
    swap.wait()
    project(1, nrm[1])

    def scores(buf, h):
        q = qtm[pl.ds(pl.multiple_of(h * 128, 128), 128)]
        s = dot(keys[:, pl.ds(pl.multiple_of((h // 8) * 128, 128), 128)], q)
        buf[...] = s
        return jnp.max(s, axis=0, keepdims=True)

    def weigh(buf, highest, h):
        p = jnp.exp2(buf[...] - highest).astype(bf16)
        o = dot(vta[pl.ds(pl.multiple_of(h * 32, 32), 32)], p)
        att[pl.ds(pl.multiple_of(h * 16, 16), 16)] = (o[:16] / o[16:17]).astype(bf16)

    def two_heads(i, highest):
        h = 2 * i
        second = scores(s_b, h + 1)
        weigh(s_a, highest, h)
        third = scores(s_a, jnp.minimum(h + 2, HEADS - 1))
        weigh(s_b, second, h + 1)
        return third

    lax.fori_loop(0, HEADS // 2, two_heads, scores(s_a, 0))

    encoded_h = (ordered + dot_tn(att[...], wout_ref[...])).astype(bf16)
    out2[...] = to_blocks(dot(comp_t[...], encoded_h)).astype(bf16)
    exchange(out2, in2, send2, recv2, loc2)

    own_row = par_ref[...] - me * POOL
    member = onehot(iota((EXT, ROWS), 0) == jnp.where(own_row < 0, POOL, own_row))
    counts = dot(member, jnp.ones((ROWS, 128), bf16))
    own_cols = jnp.transpose(jnp.broadcast_to(own_row.astype(f32), (128, ROWS)))
    member_t = jnp.concatenate([onehot(own_cols == lanes + k * 128.0) for k in range(POOL // 128)], axis=1)
    spilled = jnp.where(own_cols < 0.0, 1.0, 0.0)

    finish(out2, in2, send2, recv2, loc2)

    encoded = dot(bkt_t[...], from_blocks(in2[...]).astype(bf16)).astype(bf16)
    totals = dot(member, encoded)
    tot[...] = totals
    tal[...] = counts
    e_out[0, :, :C] = totals[POOL : POOL + 8]
    e_out[0, :, C:] = counts[POOL : POOL + 8]
    e_out[1, :, :C] = totals[POOL - 8 : POOL]
    e_out[1, :, C:] = counts[POOL - 8 : POOL]

    def edge(k, line):
        return pltpu.make_async_remote_copy(
            src_ref=e_out.at[k], dst_ref=e_in.at[k], send_sem=esend.at[k], recv_sem=erecv.at[k],
            device_id=(line // 4, line % 4), device_id_type=MESH,
        )

    to_previous = edge(0, (me + DEVS - 1) % DEVS)
    to_next = edge(1, (me + 1) % DEVS)
    to_previous.start()
    to_next.start()

    skipped = gelu(layer_norm(dot(encoded, wskip_ref[...])))

    to_previous.wait()
    to_next.wait()
    tot[POOL - 1 : POOL] += e_in[0, :1, :C]
    tal[POOL - 1 : POOL] += e_in[0, :1, C:]
    tot[POOL : POOL + 1] += e_in[1, 7:8, :C]
    tal[POOL : POOL + 1] += e_in[1, 7:8, C:]
    tallies = jnp.maximum(tal[...], 1.0)
    pooled_in = (tot[...] / jnp.concatenate([tallies, tallies], axis=1)).astype(bf16)
    pooled = gelu(layer_norm(dot(pooled_in, wpool_ref[...]))).astype(bf16)
    pooled_ref[...] = pooled[:POOL]
    lifted = gelu(layer_norm(dot(pooled, wup_ref[...]))).astype(bf16)
    picked = dot(member_t, lifted[:POOL])
    carried = lifted[POOL : POOL + 16].astype(f32)[:1]
    picked = picked + jnp.concatenate([spilled, spilled], axis=1) * carried
    dec_ref[...] = (skipped + picked).astype(bf16)


def on_device(points, to_hilbert, parent, w_qkv, w_out, w_pool, w_up, w_skip):
    vmem = pl.BlockSpec(memory_space=pltpu.VMEM)
    dma = pltpu.SemaphoreType.DMA
    return pl.pallas_call(
        kernel,
        out_shape=(
            jax.ShapeDtypeStruct((POOL, C2), bf16),
            jax.ShapeDtypeStruct((ROWS, C), bf16),
        ),
        in_specs=[vmem] * 8,
        out_specs=(vmem, vmem),
        scratch_shapes=[
            pltpu.VMEM((DEVS * BLK, 128), bf16),
            pltpu.VMEM((DEVS * BLK, 128), bf16),
            pltpu.VMEM((DEVS * BLK, 128), bf16),
            pltpu.VMEM((DEVS * BLK, 128), bf16),
            pltpu.VMEM((ROWS, SLOTS), bf16),
            pltpu.VMEM((SLOTS, ROWS), bf16),
            pltpu.VMEM((C, C), bf16),
            pltpu.VMEM((C, C), bf16),
            pltpu.VMEM((2, ROWS, C), bf16),
            pltpu.VMEM((HEADS * 128, ROWS), bf16),
            pltpu.VMEM((HEADS * 32, 2 * ROWS), bf16),
            pltpu.VMEM((2 * ROWS, C), bf16),
            pltpu.VMEM((2 * ROWS, ROWS), f32),
            pltpu.VMEM((2 * ROWS, ROWS), f32),
            pltpu.VMEM((C, ROWS), bf16),
            pltpu.VMEM((EXT, C), f32),
            pltpu.VMEM((EXT, 128), f32),
            pltpu.VMEM((2, 8, C + 128), f32),
            pltpu.VMEM((2, 8, C + 128), f32),
            dma, dma, dma, dma, dma, dma, dma, dma, dma((2,)), dma((2,)),
        ],
        compiler_params=pltpu.CompilerParams(
            collective_id=0, has_side_effects=True, vmem_limit_bytes=48 * 1024 * 1024
        ),
    )(points, to_hilbert.reshape(1, ROWS), parent.reshape(1, ROWS), w_qkv, w_out, w_pool, w_up, w_skip)


def solution(mesh):
    rows = P(("pts", "mdl"), None)
    flat = P(("pts", "mdl"))
    return jax.shard_map(
        on_device,
        mesh=mesh,
        in_specs=(rows, flat, flat, P(), P(), P(), P(), P()),
        out_specs=(rows, rows),
        check_vma=False,
    )
```

time: 222 us -> 58.7 us (0.26); the launches traced: 219 us -> 58.3 us
  waiting for transfers between devices: 59.3 us -> 0 us
  matrix products: 50.6 us -> 0 us
  Pallas kernels: 0 us -> 49.2 us
  starting transfers between devices: 38.5 us -> 0 us
  other arithmetic: 33 us -> 0 us
  local copies, waits for them, and re-layouts: 23.3 us -> 8.41 us
  between operations: 14.5 us -> 0.66 us
    dot_general x11 -> x0, matrix products: 50.6 us -> none  [the longest x2 29.9 us: attend(): jnp.einsum('hqk,khd->qhd', probs, patch_block[:, 2], preferred_element_ty...]
    pallas_call x0 -> x1, Pallas kernels: none -> 49.2 us  [on_device(): pl.pallas_call(kernel, out_shape=(jax.ShapeDtypeStruct((POOL, C2), bf16),...]
    all_to_all x4 -> x0, waiting for transfers between devices: 41.5 us -> none  [the longest x1 13 us: on_device(): lax.all_to_all(sending.reshape(devices, capacity, channels), ('pts', 'mdl...]
    all_to_all x4 -> x0, starting transfers between devices: 28.9 us -> none  [the longest x1 11.5 us: on_device(): lax.all_to_all(targets.reshape(devices, capacity), ('pts', 'mdl'), split_...]
    sub x2 -> x0, other arithmetic: 25.2 us -> none  [attend(): weights = jnp.exp(scores - highest)]
    reduce_scatter x1 -> x0, waiting for transfers between devices: 13.3 us -> none  [on_device(): lax.psum_scatter(jnp.dot(attended, head_rows, preferred_element_type=jnp....]
    scatter x3 -> x0, local copies, waits for them, and re-layouts: 10.9 us -> none  [the longest x1 4.96 us: on_device(): jnp.zeros((row_count, channels), jnp.bfloat16).at[placing]]
    ppermute x3 -> x0, starting transfers between devices: 9.44 us -> none  [passed_along(): return lax.ppermute(x, axis, pairs)]
  transfers between devices with their start and end apart: 8 -> 0, of which waited for: 7 -> 0; matrix products, arithmetic and copies ran while one was open for 7% -> 0% of each run, Pallas kernels for 0% -> 0%
where the time goes in v1:
time: 58.7 us; the launch traced here: 58.3 us
  Pallas kernels  49.2 us (84%)
  local copies, waits for them, and re-layouts  8.41 us (14%)
  between operations  0.66 us (1%)
    pallas_call x1, Pallas kernels, on_device(): pl.pallas_call(kernel, out_shape=(jax.ShapeDtypeStruct((POOL, C2), bf16),...  49.2 us
    unnamed x18, local copies, waits for them, and re-layouts  8.41 us

profile of v1, /device:TPU:1, one launch (start us, length us, event | category | flops | bytes accessed | tf_op | source)
XLA Modules:
  0.0 58.3 jit_solution(3271263881074571213)
XLA Ops:
  0.6 0.0 copy-start.6
  0.6 0.7 %copy-done.6 = s32[512]{0:T(512)S(1)} copy-done((s32[512]{0:T(512)S(1)}, s32[512]{0:T(512)}, u32[]{:S(2)}) %copy-start.6) | copy-done | bytes 2072
  1.3 0.0 copy-start
  1.3 1.0 %copy-done = bf16[256,768]{1,0:T(8,128)(2,1)S(1)} copy-done((bf16[256,768]{1,0:T(8,128)(2,1)S(1)}, bf16[256,768]{1,0:T(8,128)(2,1)}, u32[]{:S(2)}) %copy-start) | copy-done | bytes 393240
  2.3 0.0 copy-start.1
  2.3 0.9 %copy-done.1 = bf16[512,256]{1,0:T(8,128)(2,1)S(1)} copy-done((bf16[512,256]{1,0:T(8,128)(2,1)S(1)}, bf16[512,256]{1,0:T(8,128)(2,1)}, u32[]{:S(2)}) %copy-start.1) | copy-done | bytes 262168
  3.3 0.0 copy-start.2
  3.3 0.9 %copy-done.2 = bf16[256,512]{1,0:T(8,128)(2,1)S(1)} copy-done((bf16[256,512]{1,0:T(8,128)(2,1)S(1)}, bf16[256,512]{1,0:T(8,128)(2,1)}, u32[]{:S(2)}) %copy-start.2) | copy-done | bytes 262168
  4.2 0.0 copy-start.3
  4.2 0.9 %copy-done.3 = bf16[512,256]{1,0:T(8,128)(2,1)S(1)} copy-done((bf16[512,256]{1,0:T(8,128)(2,1)S(1)}, bf16[512,256]{1,0:T(8,128)(2,1)}, u32[]{:S(2)}) %copy-start.3) | copy-done | bytes 262168
  5.2 0.0 copy-start.4
  5.2 0.9 %copy-done.4 = bf16[256,256]{1,0:T(8,128)(2,1)S(1)} copy-done((bf16[256,256]{1,0:T(8,128)(2,1)S(1)}, bf16[256,256]{1,0:T(8,128)(2,1)}, u32[]{:S(2)}) %copy-start.4) | copy-done | bytes 131096
  6.1 0.0 copy-start.5
  6.1 0.9 %copy-done.5 = bf16[256,256]{1,0:T(8,128)(2,1)S(1)} copy-done((bf16[256,256]{1,0:T(8,128)(2,1)S(1)}, bf16[256,256]{1,0:T(8,128)(2,1)}, u32[]{:S(2)}) %copy-start.5) | copy-done | bytes 131096
  7.0 0.0 copy-start.7
  7.0 0.7 %copy-done.7 = s32[512]{0:T(512)S(1)} copy-done((s32[512]{0:T(512)S(1)}, s32[512]{0:T(512)}, u32[]{:S(2)}) %copy-start.7) | copy-done | bytes 2072
  7.7 49.2 %shard_map.95 = (bf16[256,512]{1,0:T(8,128)(2,1)S(1)}, bf16[512,256]{1,0:T(8,128)(2,1)S(1)}) custom-call(bf16[512,256]{1,0:T(8,128)(2,1)S(1)} %copy-done.1, s32[1,512]{1,0:T(1,128)S(1)} %bitcast.2, s32[1,512]{1,0:T(1,128)S(1)} %bitcast.3, bf16[256,768]{1,0:T(8,128)(2,1)S(1)} %copy-done, bf16[256,256]{1,0:T(8,128)(2,1)S(1)} %copy-done.4, ...), custom_call_target="tpu_custom_call" | custom-call | tf_op jit(solution)/shard_map/pallas_call | solution.py:260
  56.9 0.7 %copy.12 = bf16[256,512]{1,0:T(8,128)(2,1)} copy(bf16[256,512]{1,0:T(8,128)(2,1)S(1)} %get-tuple-element.4) | data formatting | bytes 524288
  57.6 0.7 %copy.13 = bf16[512,256]{1,0:T(8,128)(2,1)} copy(bf16[512,256]{1,0:T(8,128)(2,1)S(1)} %get-tuple-element.5) | data formatting | bytes 524288
Async XLA Ops:
  0.6 0.7 %copy-start.6 = (s32[512]{0:T(512)S(1)}, s32[512]{0:T(512)}, u32[]{:S(2)}) copy-start(s32[512]{0:T(512)} %param.9) | copy-start | bytes 6148
  1.3 1.0 %copy-start = (bf16[256,768]{1,0:T(8,128)(2,1)S(1)}, bf16[256,768]{1,0:T(8,128)(2,1)}, u32[]{:S(2)}) copy-start(bf16[256,768]{1,0:T(8,128)(2,1)} %wqkv_ref.1) | copy-start | bytes 1179652
  2.3 0.9 %copy-start.1 = (bf16[512,256]{1,0:T(8,128)(2,1)S(1)}, bf16[512,256]{1,0:T(8,128)(2,1)}, u32[]{:S(2)}) copy-start(bf16[512,256]{1,0:T(8,128)(2,1)} %pt_ref.1) | copy-start | bytes 786436
  3.3 0.9 %copy-start.2 = (bf16[256,512]{1,0:T(8,128)(2,1)S(1)}, bf16[256,512]{1,0:T(8,128)(2,1)}, u32[]{:S(2)}) copy-start(bf16[256,512]{1,0:T(8,128)(2,1)} %wpool_ref.1) | copy-start | bytes 786436
  4.2 0.9 %copy-start.3 = (bf16[512,256]{1,0:T(8,128)(2,1)S(1)}, bf16[512,256]{1,0:T(8,128)(2,1)}, u32[]{:S(2)}) copy-start(bf16[512,256]{1,0:T(8,128)(2,1)} %wup_ref.1) | copy-start | bytes 786436
  5.2 0.9 %copy-start.4 = (bf16[256,256]{1,0:T(8,128)(2,1)S(1)}, bf16[256,256]{1,0:T(8,128)(2,1)}, u32[]{:S(2)}) copy-start(bf16[256,256]{1,0:T(8,128)(2,1)} %wout_ref.1) | copy-start | bytes 393220
  6.1 0.9 %copy-start.5 = (bf16[256,256]{1,0:T(8,128)(2,1)S(1)}, bf16[256,256]{1,0:T(8,128)(2,1)}, u32[]{:S(2)}) copy-start(bf16[256,256]{1,0:T(8,128)(2,1)} %wskip_ref.1) | copy-start | bytes 393220
  7.0 0.7 %copy-start.7 = (s32[512]{0:T(512)S(1)}, s32[512]{0:T(512)}, u32[]{:S(2)}) copy-start(s32[512]{0:T(512)} %param.10) | copy-start | bytes 6148

commit v2 on v1

--- a/solution.py
+++ b/solution.py
@@ -17,7 +17,6 @@
 CAP = 8
 SLOTS = DEVS * CAP
 BLK = 2 * CAP
-EXT = POOL + 16
 EMPTY = 64.0
 QSCALE = WIDTH**-0.5 * 1.4426950408889634
 MESH = pl.DeviceIdType.MESH
@@ -75,11 +74,17 @@
 
 
 def kernel(
-    pt_ref, th_ref, par_ref, wqkv_ref, wout_ref, wpool_ref, wup_ref, wskip_ref,
-    pooled_ref, dec_ref,
-    out1, in1, out2, in2, bkt_t, comp_t, wq_t, wv_t, nrm, qtm, vta, keys, s_a, s_b, att, tot, tal, e_out, e_in,
-    send1, recv1, loc1, send2, recv2, loc2, psend, precv, esend, erecv,
+    *refs,
 ):
+    (given, (pooled_ref, dec_ref), held, rest) = refs[:8], refs[8:10], refs[10:18], refs[18:]
+    pt_ref, th_ref, par_ref, wqkv_ref, wout_ref, wpool_ref, wup_ref, wskip_ref = held
+    (
+    out1, in1, out2, in2, bkt_t, comp_t, wq_t, wv_t, nrm, qtm, vta, keys, s_a, s_b, att, e_out, e_in,
+    send1, recv1, loc1, send2, recv2, loc2, psend, precv, esend, erecv, fetched,
+    ) = rest
+    loads = [pltpu.make_async_copy(given[i], held[i], fetched.at[i]) for i in range(8)]
+    for i in (1, 0, 2, 3, 4, 7, 5, 6):
+        loads[i].start()
     pts, mdl = lax.axis_index("pts"), lax.axis_index("mdl")
     me = pts * 4 + mdl
     core, yy, xx = pts % 2, (pts // 2) % 4, pts // 8
@@ -98,6 +103,7 @@
     for o in OFFSETS:
         pl.semaphore_signal(barrier, inc=1, device_id=place(o), device_id_type=MESH)
 
+    loads[1].wait()
     half = th_ref[...] >> 9
     target = (half >> 3) * 8 + (half & 1) * 4 + ((half >> 1) & 3)
     match = jnp.where(iota((DEVS, ROWS), 0) == target, 1.0, 0.0)
@@ -107,7 +113,9 @@
     slot = target * CAP + rank.astype(i32)
     bucket = jnp.where(iota((SLOTS, ROWS), 0) == slot, 1.0, 0.0)
     taken = jnp.sum(bucket, axis=1, keepdims=True)
-    filled = dot(bucket.astype(bf16), pt_ref[...])
+    loads[0].wait()
+    normed = layer_norm(pt_ref[...].astype(f32)).astype(bf16)
+    filled = dot(bucket.astype(bf16), normed)
     lane = iota((1, C), 1)
     filled = filled + jnp.where(lane < 128, (1.0 - taken) * EMPTY, 0.0)
     out1[...] = to_blocks(filled).astype(bf16)
@@ -140,24 +148,33 @@
     lanes = iota((1, 128), 1).astype(f32)
     for k in range(SLOTS // 128):
         bkt_t[:, k * 128 : (k + 1) * 128] = onehot(slot_cols == lanes + k * 128.0)
+    for i in range(2, 8):
+        loads[i].wait()
     wq_t[...] = jnp.transpose(wqkv_ref[:, :C])
     wv_t[...] = jnp.transpose(wqkv_ref[:, 2 * C :])
     qtm[...] = jnp.zeros_like(qtm)
     for h in range(HEADS):
         vta[32 * h + 16 : 32 * h + 32] = jnp.ones((16, 2 * ROWS), bf16)
-    lower = onehot(iota((SLOTS, SLOTS), 1) < iota((SLOTS, SLOTS), 0))
+    sublane = iota((DEVS, CAP, 128), 1).astype(f32)
+    pick = jnp.where(iota((16, 128), 1) == 0, 32.0, jnp.where(iota((16, 128), 1) == 64, 1.0, 0.0)).astype(bf16)
 
     finish(out1, in1, send1, recv1, loc1)
 
-    arrived = from_blocks(in1[...])
-    valid = jnp.broadcast_to(jnp.where(arrived[:, :1] < 32.0, 1.0, 0.0), (SLOTS, 128))
-    place_of = jnp.where(valid > 0.0, dot(lower, valid.astype(bf16)), -1.0)
-    for k in range(ROWS // 128):
-        comp_t[:, k * 128 : (k + 1) * 128] = onehot(place_of == lanes + k * 128.0)
-    place_row = jnp.transpose(place_of)[:1].astype(i32)
+    halves = in1[...].astype(f32).reshape(DEVS, BLK, 128)
+    valid = jnp.where(halves[:, :CAP] < 32.0, 1.0, 0.0)
+    base = jnp.sum(valid, axis=1, keepdims=True)
+    step = 1
+    while step < DEVS:
+        base = base + jnp.concatenate([jnp.zeros((step, 1, 128), f32), base[:-step]], axis=0)
+        step *= 2
+    base = base - jnp.sum(valid, axis=1, keepdims=True)
+    place_of = jnp.where(valid > 0.0, base + sublane, -1.0).reshape(SLOTS, 128)
+    high = jnp.floor(place_of * (1.0 / 32.0))
+    digits = jnp.where(iota((SLOTS, 128), 1) < 64, high, place_of - 32.0 * high).astype(bf16)
+    place_row = dot_nt(pick, digits)[:1].astype(i32)
     comp = onehot(iota((ROWS, SLOTS), 0) == place_row)
-    ordered = dot(comp, arrived.astype(bf16))
-    normed = layer_norm(ordered).astype(bf16)
+    arrived = jnp.concatenate([halves[:, :CAP], halves[:, CAP:]], axis=2).reshape(SLOTS, C).astype(bf16)
+    normed = dot(comp, arrived).astype(bf16)
     nrm[0] = normed
 
     swap = pltpu.make_async_remote_copy(
@@ -166,6 +183,8 @@
     )
     swap.start()
 
+    for k in range(ROWS // 128):
+        comp_t[:, k * 128 : (k + 1) * 128] = onehot(place_of == lanes + k * 128.0)
     queries = (dot_nt(wq_t[...], normed) * QSCALE).astype(bf16)
     for h in range(HEADS):
         low = h * 128 + (16 * h) % 128
@@ -202,27 +221,33 @@
 
     lax.fori_loop(0, HEADS // 2, two_heads, scores(s_a, 0))
 
-    encoded_h = (ordered + dot_tn(att[...], wout_ref[...])).astype(bf16)
-    out2[...] = to_blocks(dot(comp_t[...], encoded_h)).astype(bf16)
+    attended = jnp.transpose(att[...])
+    out2[...] = to_blocks(dot(comp_t[...], attended)).astype(bf16)
     exchange(out2, in2, send2, recv2, loc2)
 
     own_row = par_ref[...] - me * POOL
-    member = onehot(iota((EXT, ROWS), 0) == jnp.where(own_row < 0, POOL, own_row))
-    counts = dot(member, jnp.ones((ROWS, 128), bf16))
+    member = onehot(iota((POOL, ROWS), 0) == own_row)
+    ones = jnp.ones((ROWS, 128), bf16)
+    counts = jnp.maximum(dot(member, ones), 1.0)
+    edge_member = onehot(jnp.where(iota((16, ROWS), 0) < 8, -1, POOL - 1) == own_row)
+    edge_counts = dot(edge_member, ones)
     own_cols = jnp.transpose(jnp.broadcast_to(own_row.astype(f32), (128, ROWS)))
-    member_t = jnp.concatenate([onehot(own_cols == lanes + k * 128.0) for k in range(POOL // 128)], axis=1)
-    spilled = jnp.where(own_cols < 0.0, 1.0, 0.0)
+    inner_t = jnp.concatenate(
+        [onehot(jnp.where(own_cols == POOL - 1.0, -1.0, own_cols) == lanes + k * 128.0) for k in range(POOL // 128)],
+        axis=1,
+    )
+    last_cols = jnp.where(own_cols == POOL - 1.0, 1.0, 0.0)
+    spilled_cols = jnp.where(own_cols < 0.0, 1.0, 0.0)
+    for k in range(2):
+        e_out[k, :, C:] = edge_counts[8 * k : 8 * k + 8]
 
     finish(out2, in2, send2, recv2, loc2)
 
-    encoded = dot(bkt_t[...], from_blocks(in2[...]).astype(bf16)).astype(bf16)
-    totals = dot(member, encoded)
-    tot[...] = totals
-    tal[...] = counts
-    e_out[0, :, :C] = totals[POOL : POOL + 8]
-    e_out[0, :, C:] = counts[POOL : POOL + 8]
-    e_out[1, :, :C] = totals[POOL - 8 : POOL]
-    e_out[1, :, C:] = counts[POOL - 8 : POOL]
+    attended = dot(bkt_t[...], from_blocks(in2[...]).astype(bf16)).astype(bf16)
+    encoded = (pt_ref[...].astype(f32) + dot(attended, wout_ref[...])).astype(bf16)
+    edge_sums = dot(edge_member, encoded)
+    for k in range(2):
+        e_out[k, :, :C] = edge_sums[8 * k : 8 * k + 8]
 
     def edge(k, line):
         return pltpu.make_async_remote_copy(
@@ -235,37 +260,57 @@
     to_previous.start()
     to_next.start()
 
+    def pool(sums, tallies):
+        mean = sums / jnp.concatenate([tallies, tallies], axis=1)
+        return gelu(layer_norm(dot(mean.astype(bf16), wpool_ref[...]))).astype(bf16)
+
+    def lift(rows):
+        return gelu(layer_norm(dot(rows, wup_ref[...]))).astype(bf16)
+
+    pooled = pool(dot(member, encoded), counts)
+    pooled_ref[...] = pooled
     skipped = gelu(layer_norm(dot(encoded, wskip_ref[...])))
+    partial = skipped + dot(inner_t, lift(pooled))
 
     to_previous.wait()
     to_next.wait()
-    tot[POOL - 1 : POOL] += e_in[0, :1, :C]
-    tal[POOL - 1 : POOL] += e_in[0, :1, C:]
-    tot[POOL : POOL + 1] += e_in[1, 7:8, :C]
-    tal[POOL : POOL + 1] += e_in[1, 7:8, C:]
-    tallies = jnp.maximum(tal[...], 1.0)
-    pooled_in = (tot[...] / jnp.concatenate([tallies, tallies], axis=1)).astype(bf16)
-    pooled = gelu(layer_norm(dot(pooled_in, wpool_ref[...]))).astype(bf16)
-    pooled_ref[...] = pooled[:POOL]
-    lifted = gelu(layer_norm(dot(pooled, wup_ref[...]))).astype(bf16)
-    picked = dot(member_t, lifted[:POOL])
-    carried = lifted[POOL : POOL + 16].astype(f32)[:1]
-    picked = picked + jnp.concatenate([spilled, spilled], axis=1) * carried
-    dec_ref[...] = (skipped + picked).astype(bf16)
+    shared = jnp.concatenate([e_out[1] + e_in[0], e_in[1] + e_out[0]], axis=0)
+    shared_pooled = pool(shared[:, :C], jnp.maximum(shared[:, C:], 1.0))
+    pooled_ref[POOL - 16 :] = jnp.where(iota((16, C2), 0) == 15, shared_pooled[:1], pooled[POOL - 16 :])
+    shared_lifted = lift(shared_pooled).astype(f32)
+    both = lambda v: jnp.concatenate([v, v], axis=1)
+    picked = both(last_cols) * shared_lifted[:1] + both(spilled_cols) * shared_lifted[8:9]
+    dec_ref[...] = (partial + picked).astype(bf16)
+
+
+def hand_out(pooled_ref, dec_ref, pooled_out, dec_out, sems):
+    first = pltpu.make_async_copy(dec_ref, dec_out, sems.at[0])
+    second = pltpu.make_async_copy(pooled_ref, pooled_out, sems.at[1])
+    first.start()
+    second.start()
+    first.wait()
+    second.wait()
 
 
 def on_device(points, to_hilbert, parent, w_qkv, w_out, w_pool, w_up, w_skip):
+    given = (points, to_hilbert.reshape(1, ROWS), parent.reshape(1, ROWS), w_qkv, w_out, w_pool, w_up, w_skip)
     vmem = pl.BlockSpec(memory_space=pltpu.VMEM)
     dma = pltpu.SemaphoreType.DMA
-    return pl.pallas_call(
+    held = [pltpu.with_memory_space_constraint(v, pltpu.HBM) for v in given]
+    results = pl.pallas_call(
         kernel,
-        out_shape=(
-            jax.ShapeDtypeStruct((POOL, C2), bf16),
-            jax.ShapeDtypeStruct((ROWS, C), bf16),
-        ),
-        in_specs=[vmem] * 8,
+        out_shape=(pltpu.VMEM((POOL, C2), bf16), pltpu.VMEM((ROWS, C), bf16)),
+        in_specs=[pl.BlockSpec(memory_space=pltpu.HBM)] * 8,
         out_specs=(vmem, vmem),
         scratch_shapes=[
+            pltpu.VMEM((ROWS, C), bf16),
+            pltpu.VMEM((1, ROWS), i32),
+            pltpu.VMEM((1, ROWS), i32),
+            pltpu.VMEM((C, 3 * C), bf16),
+            pltpu.VMEM((C, C), bf16),
+            pltpu.VMEM((C, C2), bf16),
+            pltpu.VMEM((C2, C), bf16),
+            pltpu.VMEM((C, C), bf16),
             pltpu.VMEM((DEVS * BLK, 128), bf16),
             pltpu.VMEM((DEVS * BLK, 128), bf16),
             pltpu.VMEM((DEVS * BLK, 128), bf16),
@@ -281,16 +326,22 @@
             pltpu.VMEM((2 * ROWS, ROWS), f32),
             pltpu.VMEM((2 * ROWS, ROWS), f32),
             pltpu.VMEM((C, ROWS), bf16),
-            pltpu.VMEM((EXT, C), f32),
-            pltpu.VMEM((EXT, 128), f32),
             pltpu.VMEM((2, 8, C + 128), f32),
             pltpu.VMEM((2, 8, C + 128), f32),
-            dma, dma, dma, dma, dma, dma, dma, dma, dma((2,)), dma((2,)),
+            dma, dma, dma, dma, dma, dma, dma, dma, dma((2,)), dma((2,)), dma((8,)),
         ],
         compiler_params=pltpu.CompilerParams(
             collective_id=0, has_side_effects=True, vmem_limit_bytes=48 * 1024 * 1024
         ),
-    )(points, to_hilbert.reshape(1, ROWS), parent.reshape(1, ROWS), w_qkv, w_out, w_pool, w_up, w_skip)
+    )(*held)
+    anywhere = pl.BlockSpec(memory_space=pl.ANY)
+    return pl.pallas_call(
+        hand_out,
+        out_shape=(jax.ShapeDtypeStruct((POOL, C2), bf16), jax.ShapeDtypeStruct((ROWS, C), bf16)),
+        in_specs=[anywhere, anywhere],
+        out_specs=(anywhere, anywhere),
+        scratch_shapes=[dma((2,))],
+    )(*results)
 
 
 def solution(mesh):

time: 58.7 us -> 67.4 us (1.15)
  Pallas kernels: 49.2 us -> 65.1 us
  local copies, waits for them, and re-layouts: 8.41 us -> 1.39 us
    pallas_call x1 -> x2, Pallas kernels: 49.2 us -> 65.1 us  [the longest x1 48.1 us: on_device(): pl.pallas_call(kernel, out_shape=(pltpu.VMEM((POOL, C2), bf16), pltpu.VME...]
    unnamed x18 -> x4, local copies, waits for them, and re-layouts: 8.41 us -> 1.39 us
where the time goes in v2:
time: 67.4 us; the launch traced here: 67.1 us
  Pallas kernels  65.1 us (97%)
  local copies, waits for them, and re-layouts  1.39 us (2%)
    pallas_call x1, Pallas kernels, on_device(): pl.pallas_call(kernel, out_shape=(pltpu.VMEM((POOL, C2), bf16), pltpu.VME...  48.1 us
    pallas_call x1, Pallas kernels, on_device(): pl.pallas_call(hand_out, out_shape=(jax.ShapeDtypeStruct((POOL, C2), bf16...  17 us
    unnamed x4, local copies, waits for them, and re-layouts  1.39 us

profile of v2, /device:TPU:1, one launch (start us, length us, event | category | flops | bytes accessed | tf_op | source)
XLA Modules:
  0.0 67.1 jit_solution(11826877366369857627)
XLA Ops:
  0.6 48.1 %shard_map.95 = (bf16[256,512]{1,0:T(8,128)(2,1)S(1)}, bf16[512,256]{1,0:T(8,128)(2,1)S(1)}) custom-call(bf16[512,256]{1,0:T(8,128)(2,1)} %refs_0_.1, s32[1,512]{1,0:T(1,128)} %bitcast.2, s32[1,512]{1,0:T(1,128)} %bitcast.3, bf16[256,768]{1,0:T(8,128)(2,1)} %refs_3_.1, bf16[256,256]{1,0:T(8,128)(2,1)} %refs_4_.1, bf16[256,512]{1,0:T(8,128)(2,1)} %refs_5_.1, ...), custom_call_target="tpu_custom_call" | custom-call | tf_op jit(solution)/shard_map/pallas_call | solution.py:300
  48.7 0.0 copy-start
  48.7 0.7 %copy-done = bf16[256,512]{1,0:T(8,128)(2,1)} copy-done((bf16[256,512]{1,0:T(8,128)(2,1)}, bf16[256,512]{1,0:T(8,128)(2,1)S(1)}, u32[]{:S(2)}) %copy-start) | copy-done | bytes 262168
  49.4 0.0 copy-start.1
  49.4 0.7 %copy-done.1 = bf16[512,256]{1,0:T(8,128)(2,1)} copy-done((bf16[512,256]{1,0:T(8,128)(2,1)}, bf16[512,256]{1,0:T(8,128)(2,1)S(1)}, u32[]{:S(2)}) %copy-start.1) | copy-done | bytes 262168
  50.1 17.0 %shard_map.96 = (bf16[256,512]{1,0:T(8,128)(2,1)}, bf16[512,256]{1,0:T(8,128)(2,1)}) custom-call(bf16[256,512]{1,0:T(8,128)(2,1)} %copy-done, bf16[512,256]{1,0:T(8,128)(2,1)} %copy-done.1), custom_call_target="tpu_custom_call" | custom-call | tf_op jit(solution)/shard_map/pallas_call | solution.py:338
Async XLA Ops:
  48.7 0.7 %copy-start = (bf16[256,512]{1,0:T(8,128)(2,1)}, bf16[256,512]{1,0:T(8,128)(2,1)S(1)}, u32[]{:S(2)}) copy-start(bf16[256,512]{1,0:T(8,128)(2,1)S(1)} %get-tuple-element.4.pooled_ref) | copy-start | bytes 786436
  49.4 0.7 %copy-start.1 = (bf16[512,256]{1,0:T(8,128)(2,1)}, bf16[512,256]{1,0:T(8,128)(2,1)S(1)}, u32[]{:S(2)}) copy-start(bf16[512,256]{1,0:T(8,128)(2,1)S(1)} %get-tuple-element.5.dec_ref) | copy-start | bytes 786436

commit v3 on v2

--- a/solution.py
+++ b/solution.py
@@ -68,11 +68,6 @@
     return jnp.concatenate([v[:, :, :128], v[:, :, 128:]], axis=1).reshape(DEVS * BLK, 128)
 
 
-def from_blocks(b):
-    v = b.astype(f32).reshape(DEVS, BLK, 128)
-    return jnp.concatenate([v[:, :CAP], v[:, CAP:]], axis=2).reshape(SLOTS, C)
-
-
 def kernel(
     *refs,
 ):
@@ -83,8 +78,6 @@
     send1, recv1, loc1, send2, recv2, loc2, psend, precv, esend, erecv, fetched,
     ) = rest
     loads = [pltpu.make_async_copy(given[i], held[i], fetched.at[i]) for i in range(8)]
-    for i in (1, 0, 2, 3, 4, 7, 5, 6):
-        loads[i].start()
     pts, mdl = lax.axis_index("pts"), lax.axis_index("mdl")
     me = pts * 4 + mdl
     core, yy, xx = pts % 2, (pts // 2) % 4, pts // 8
@@ -100,8 +93,11 @@
         return pl.ds(pl.multiple_of(line * BLK, BLK), BLK)
 
     barrier = pltpu.get_barrier_semaphore()
-    for o in OFFSETS:
+    for k, o in enumerate(OFFSETS):
         pl.semaphore_signal(barrier, inc=1, device_id=place(o), device_id_type=MESH)
+        if k == 15:
+            for i in (1, 0, 2, 3, 4, 7, 5, 6):
+                loads[i].start()
 
     loads[1].wait()
     half = th_ref[...] >> 9
@@ -153,8 +149,6 @@
     wq_t[...] = jnp.transpose(wqkv_ref[:, :C])
     wv_t[...] = jnp.transpose(wqkv_ref[:, 2 * C :])
     qtm[...] = jnp.zeros_like(qtm)
-    for h in range(HEADS):
-        vta[32 * h + 16 : 32 * h + 32] = jnp.ones((16, 2 * ROWS), bf16)
     sublane = iota((DEVS, CAP, 128), 1).astype(f32)
     pick = jnp.where(iota((16, 128), 1) == 0, 32.0, jnp.where(iota((16, 128), 1) == 64, 1.0, 0.0)).astype(bf16)
 
@@ -193,8 +187,7 @@
     def project(part, rows):
         keys[part * ROWS : (part + 1) * ROWS] = dot(rows, wqkv_ref[:, C : 2 * C]).astype(bf16)
         values = dot_nt(wv_t[...], rows).astype(bf16)
-        for h in range(HEADS):
-            vta[32 * h : 32 * h + 16, part * ROWS : (part + 1) * ROWS] = values[16 * h : 16 * h + 16]
+        vta[:, part * ROWS : (part + 1) * ROWS] = values
 
     project(0, normed)
     swap.wait()
@@ -207,9 +200,11 @@
         return jnp.max(s, axis=0, keepdims=True)
 
     def weigh(buf, highest, h):
-        p = jnp.exp2(buf[...] - highest).astype(bf16)
-        o = dot(vta[pl.ds(pl.multiple_of(h * 32, 32), 32)], p)
-        att[pl.ds(pl.multiple_of(h * 16, 16), 16)] = (o[:16] / o[16:17]).astype(bf16)
+        weights = jnp.exp2(buf[...] - highest)
+        total = jnp.sum(weights, axis=0, keepdims=True)
+        p = weights.astype(bf16)
+        o = dot(vta[pl.ds(pl.multiple_of(h * WIDTH, WIDTH), WIDTH)], p)
+        att[pl.ds(pl.multiple_of(h * WIDTH, WIDTH), WIDTH)] = (o / total).astype(bf16)
 
     def two_heads(i, highest):
         h = 2 * i
@@ -219,11 +214,38 @@
         weigh(s_b, second, h + 1)
         return third
 
-    lax.fori_loop(0, HEADS // 2, two_heads, scores(s_a, 0))
-
-    attended = jnp.transpose(att[...])
-    out2[...] = to_blocks(dot(comp_t[...], attended)).astype(bf16)
-    exchange(out2, in2, send2, recv2, loc2)
+    def back(half):
+        rows = jnp.transpose(att[half * 128 : (half + 1) * 128])
+        out2[half] = dot(comp_t[...], rows).reshape(DEVS, CAP, 128).astype(bf16)
+        pltpu.make_async_copy(out2.at[half, me], in2.at[half, me], loc2.at[half]).start()
+
+        def send(o):
+            p, m = place(o)
+            pltpu.make_async_remote_copy(
+                src_ref=out2.at[half, p * 4 + m],
+                dst_ref=in2.at[half, me],
+                send_sem=send2.at[half],
+                recv_sem=recv2.at[half],
+                device_id=(p, m),
+                device_id_type=MESH,
+            ).start()
+
+        return [functools.partial(send, o) for o in OFFSETS]
+
+    def back_wait(half):
+        pltpu.make_async_copy(out2.at[half, 0], in2.at[half, 0], loc2.at[half]).wait()
+        pltpu.make_async_copy(out2.at[half, : DEVS - 1], out2.at[half, : DEVS - 1], send2.at[half]).wait()
+        pltpu.make_async_copy(in2.at[half, : DEVS - 1], in2.at[half, : DEVS - 1], recv2.at[half]).wait()
+        return in2[half].astype(f32).reshape(SLOTS, 128).astype(bf16)
+
+    quarter = HEADS // 4
+    highest = lax.fori_loop(0, quarter, two_heads, scores(s_a, 0))
+    sends = back(0)
+    for send in sends:
+        send()
+    lax.fori_loop(quarter, 2 * quarter, two_heads, highest)
+    for send in back(1):
+        send()
 
     own_row = par_ref[...] - me * POOL
     member = onehot(iota((POOL, ROWS), 0) == own_row)
@@ -241,9 +263,8 @@
     for k in range(2):
         e_out[k, :, C:] = edge_counts[8 * k : 8 * k + 8]
 
-    finish(out2, in2, send2, recv2, loc2)
-
-    attended = dot(bkt_t[...], from_blocks(in2[...]).astype(bf16)).astype(bf16)
+    attended = [dot(bkt_t[...], back_wait(half)).astype(bf16) for half in range(2)]
+    attended = jnp.concatenate(attended, axis=1)
     encoded = (pt_ref[...].astype(f32) + dot(attended, wout_ref[...])).astype(bf16)
     edge_sums = dot(edge_member, encoded)
     for k in range(2):
@@ -313,32 +334,33 @@
             pltpu.VMEM((C, C), bf16),
             pltpu.VMEM((DEVS * BLK, 128), bf16),
             pltpu.VMEM((DEVS * BLK, 128), bf16),
-            pltpu.VMEM((DEVS * BLK, 128), bf16),
-            pltpu.VMEM((DEVS * BLK, 128), bf16),
+            pltpu.VMEM((2, DEVS, CAP, 128), bf16),
+            pltpu.VMEM((2, DEVS, CAP, 128), bf16),
             pltpu.VMEM((ROWS, SLOTS), bf16),
             pltpu.VMEM((SLOTS, ROWS), bf16),
             pltpu.VMEM((C, C), bf16),
             pltpu.VMEM((C, C), bf16),
             pltpu.VMEM((2, ROWS, C), bf16),
             pltpu.VMEM((HEADS * 128, ROWS), bf16),
-            pltpu.VMEM((HEADS * 32, 2 * ROWS), bf16),
+            pltpu.VMEM((C, 2 * ROWS), bf16),
             pltpu.VMEM((2 * ROWS, C), bf16),
             pltpu.VMEM((2 * ROWS, ROWS), f32),
             pltpu.VMEM((2 * ROWS, ROWS), f32),
             pltpu.VMEM((C, ROWS), bf16),
             pltpu.VMEM((2, 8, C + 128), f32),
             pltpu.VMEM((2, 8, C + 128), f32),
-            dma, dma, dma, dma, dma, dma, dma, dma, dma((2,)), dma((2,)), dma((8,)),
+            dma, dma, dma, dma((2,)), dma((2,)), dma((2,)), dma, dma, dma((2,)), dma((2,)), dma((8,)),
         ],
         compiler_params=pltpu.CompilerParams(
             collective_id=0, has_side_effects=True, vmem_limit_bytes=48 * 1024 * 1024
         ),
     )(*held)
+    results = [pltpu.with_memory_space_constraint(v, pltpu.VMEM) for v in results]
     anywhere = pl.BlockSpec(memory_space=pl.ANY)
     return pl.pallas_call(
         hand_out,
         out_shape=(jax.ShapeDtypeStruct((POOL, C2), bf16), jax.ShapeDtypeStruct((ROWS, C), bf16)),
-        in_specs=[anywhere, anywhere],
+        in_specs=[vmem, vmem],
         out_specs=(anywhere, anywhere),
         scratch_shapes=[dma((2,))],
     )(*results)

time: 67.4 us -> 46.7 us (0.69)
  Pallas kernels: 65.1 us -> 45.9 us
  local copies, waits for them, and re-layouts: 1.39 us -> 0 us
    pallas_call x1, Pallas kernels: 17 us -> 0.81 us  [on_device(): pl.pallas_call(hand_out, out_shape=(jax.ShapeDtypeStruct((POOL, C2), bf16...]
    pallas_call x1, Pallas kernels: 48.1 us -> 45.1 us  [on_device(): pl.pallas_call(kernel, out_shape=(pltpu.VMEM((POOL, C2), bf16), pltpu.VME...]
    unnamed x4 -> x0, local copies, waits for them, and re-layouts: 1.39 us -> none
where the time goes in v3:
time: 46.7 us; the launch traced here: 46.6 us
  Pallas kernels  45.9 us (98%)
  between operations  0.64 us (1%)
    pallas_call x1, Pallas kernels, on_device(): pl.pallas_call(kernel, out_shape=(pltpu.VMEM((POOL, C2), bf16), pltpu.VME...  45.1 us

profile of v3, /device:TPU:1, one launch (start us, length us, event | category | flops | bytes accessed | tf_op | source)
XLA Modules:
  0.0 46.6 jit_solution(11577620122525212451)
XLA Ops:
  0.6 45.1 %shard_map.95 = (bf16[256,512]{1,0:T(8,128)(2,1)S(1)}, bf16[512,256]{1,0:T(8,128)(2,1)S(1)}) custom-call(bf16[512,256]{1,0:T(8,128)(2,1)} %refs_0_.1, s32[1,512]{1,0:T(1,128)} %bitcast.2, s32[1,512]{1,0:T(1,128)} %bitcast.3, bf16[256,768]{1,0:T(8,128)(2,1)} %refs_3_.1, bf16[256,256]{1,0:T(8,128)(2,1)} %refs_4_.1, bf16[256,512]{1,0:T(8,128)(2,1)} %refs_5_.1, ...), custom_call_target="tpu_custom_call" | custom-call | tf_op jit(solution)/shard_map/pallas_call | solution.py:321
  45.8 0.8 %shard_map.96 = (bf16[256,512]{1,0:T(8,128)(2,1)}, bf16[512,256]{1,0:T(8,128)(2,1)}) custom-call(bf16[256,512]{1,0:T(8,128)(2,1)S(1)} %get-tuple-element.4.pooled_ref, bf16[512,256]{1,0:T(8,128)(2,1)S(1)} %get-tuple-element.5.dec_ref), custom_call_target="tpu_custom_call" | custom-call | tf_op jit(solution)/shard_map/pallas_call | solution.py:360

commit v4 on v2

--- a/solution.py
+++ b/solution.py
@@ -31,6 +31,12 @@
 
 
 OFFSETS = _offsets()
+FIRST = 32
+QUERIES = FIRST * CAP
+
+
+def minus(o):
+    return tuple((-v) % (2 if k == 2 else 4) for k, v in enumerate(o))
 
 
 def dot(a, b):
@@ -66,11 +72,6 @@
 def to_blocks(v):
     v = v.reshape(DEVS, CAP, C)
     return jnp.concatenate([v[:, :, :128], v[:, :, 128:]], axis=1).reshape(DEVS * BLK, 128)
-
-
-def from_blocks(b):
-    v = b.astype(f32).reshape(DEVS, BLK, 128)
-    return jnp.concatenate([v[:, :CAP], v[:, CAP:]], axis=2).reshape(SLOTS, C)
 
 
 def kernel(
@@ -79,12 +80,10 @@
     (given, (pooled_ref, dec_ref), held, rest) = refs[:8], refs[8:10], refs[10:18], refs[18:]
     pt_ref, th_ref, par_ref, wqkv_ref, wout_ref, wpool_ref, wup_ref, wskip_ref = held
     (
-    out1, in1, out2, in2, bkt_t, comp_t, wq_t, wv_t, nrm, qtm, vta, keys, s_a, s_b, att, e_out, e_in,
+    out1, in1, out2, in2, bkt_t, comp_t, wq_t, wv_t, nrm, qtm, vta, keys, s_0, s_1, s_2, s_3, att, part_o, part_l, part_m, e_out, e_in,
     send1, recv1, loc1, send2, recv2, loc2, psend, precv, esend, erecv, fetched,
     ) = rest
     loads = [pltpu.make_async_copy(given[i], held[i], fetched.at[i]) for i in range(8)]
-    for i in (1, 0, 2, 3, 4, 7, 5, 6):
-        loads[i].start()
     pts, mdl = lax.axis_index("pts"), lax.axis_index("mdl")
     me = pts * 4 + mdl
     core, yy, xx = pts % 2, (pts // 2) % 4, pts // 8
@@ -100,8 +99,11 @@
         return pl.ds(pl.multiple_of(line * BLK, BLK), BLK)
 
     barrier = pltpu.get_barrier_semaphore()
-    for o in OFFSETS:
+    for k, o in enumerate(OFFSETS):
         pl.semaphore_signal(barrier, inc=1, device_id=place(o), device_id_type=MESH)
+        if k == 15:
+            for i in (1, 0, 2, 3, 4, 7, 5, 6):
+                loads[i].start()
 
     loads[1].wait()
     half = th_ref[...] >> 9
@@ -122,27 +124,19 @@
 
     pl.semaphore_wait(barrier, DEVS - 1)
 
-    def exchange(src, dst, send, recv, loc):
-        own = pltpu.make_async_copy(src.at[block(me)], dst.at[block(me)], loc)
-        for o in OFFSETS:
-            p, m = place(o)
-            pltpu.make_async_remote_copy(
-                src_ref=src.at[block(p * 4 + m)],
-                dst_ref=dst.at[block(me)],
-                send_sem=send,
-                recv_sem=recv,
-                device_id=(p, m),
-                device_id_type=MESH,
-            ).start()
-        own.start()
-
-    def finish(src, dst, send, recv, loc):
-        most = pl.ds(0, (DEVS - 1) * BLK)
-        pltpu.make_async_copy(src.at[block(0)], dst.at[block(0)], loc).wait()
-        pltpu.make_async_copy(src.at[most], src.at[most], send).wait()
-        pltpu.make_async_copy(dst.at[most], dst.at[most], recv).wait()
-
-    exchange(out1, in1, send1, recv1, loc1)
+    last = (DEVS - 1) * BLK
+    own = pltpu.make_async_copy(out1.at[block(me)], in1.at[pl.ds(last, BLK)], loc1)
+    own.start()
+    for o in OFFSETS:
+        p, m = place(o)
+        pltpu.make_async_remote_copy(
+            src_ref=out1.at[block(p * 4 + m)],
+            dst_ref=in1.at[pl.ds(OFFSETS.index(minus(o)) * BLK, BLK)],
+            send_sem=send1,
+            recv_sem=recv1,
+            device_id=(p, m),
+            device_id_type=MESH,
+        ).start()
 
     slot_cols = jnp.transpose(jnp.broadcast_to(slot.astype(f32), (128, ROWS)))
     lanes = iota((1, 128), 1).astype(f32)
@@ -153,22 +147,19 @@
     wq_t[...] = jnp.transpose(wqkv_ref[:, :C])
     wv_t[...] = jnp.transpose(wqkv_ref[:, 2 * C :])
     qtm[...] = jnp.zeros_like(qtm)
-    for h in range(HEADS):
-        vta[32 * h + 16 : 32 * h + 32] = jnp.ones((16, 2 * ROWS), bf16)
     sublane = iota((DEVS, CAP, 128), 1).astype(f32)
     pick = jnp.where(iota((16, 128), 1) == 0, 32.0, jnp.where(iota((16, 128), 1) == 64, 1.0, 0.0)).astype(bf16)
 
-    finish(out1, in1, send1, recv1, loc1)
-
+    own.wait()
+    came = in1.at[pl.ds(0, last)]
+    pltpu.make_async_copy(came, came, recv1).wait()
     halves = in1[...].astype(f32).reshape(DEVS, BLK, 128)
     valid = jnp.where(halves[:, :CAP] < 32.0, 1.0, 0.0)
-    base = jnp.sum(valid, axis=1, keepdims=True)
-    step = 1
-    while step < DEVS:
-        base = base + jnp.concatenate([jnp.zeros((step, 1, 128), f32), base[:-step]], axis=0)
-        step *= 2
-    base = base - jnp.sum(valid, axis=1, keepdims=True)
-    place_of = jnp.where(valid > 0.0, base + sublane, -1.0).reshape(SLOTS, 128)
+    counts = jnp.sum(valid, axis=1, keepdims=True)
+    upto = counts
+    for step in (1, 2, 4, 8, 16, 32, 64):
+        upto = upto + jnp.concatenate([jnp.zeros((step, 1, 128), f32), upto[:-step]], axis=0)
+    place_of = jnp.where(valid > 0.0, upto - counts + sublane, -1.0).reshape(SLOTS, 128)
     high = jnp.floor(place_of * (1.0 / 32.0))
     digits = jnp.where(iota((SLOTS, 128), 1) < 64, high, place_of - 32.0 * high).astype(bf16)
     place_row = dot_nt(pick, digits)[:1].astype(i32)
@@ -183,8 +174,8 @@
     )
     swap.start()
 
-    for k in range(ROWS // 128):
-        comp_t[:, k * 128 : (k + 1) * 128] = onehot(place_of == lanes + k * 128.0)
+    for c in range(ROWS // 128):
+        comp_t[:, c * 128 : (c + 1) * 128] = onehot(place_of == lanes + c * 128.0)
     queries = (dot_nt(wq_t[...], normed) * QSCALE).astype(bf16)
     for h in range(HEADS):
         low = h * 128 + (16 * h) % 128
@@ -193,37 +184,103 @@
     def project(part, rows):
         keys[part * ROWS : (part + 1) * ROWS] = dot(rows, wqkv_ref[:, C : 2 * C]).astype(bf16)
         values = dot_nt(wv_t[...], rows).astype(bf16)
-        for h in range(HEADS):
-            vta[32 * h : 32 * h + 16, part * ROWS : (part + 1) * ROWS] = values[16 * h : 16 * h + 16]
+        vta[:, part * ROWS : (part + 1) * ROWS] = values
 
     project(0, normed)
+
+    even, odd = (s_0, s_1), (s_2, s_3)
+
+    def queries_of(u):
+        return pl.ds(pl.multiple_of(u // 8 * QUERIES, QUERIES), QUERIES)
+
+    def scores(bufs, u, low, count):
+        highest = []
+        for k, buf in enumerate(bufs):
+            h = u % 8 * 2 + k
+            q = qtm[pl.ds(pl.multiple_of(h * 128, 128), 128), queries_of(u)]
+            s = dot(keys[low : low + count, pl.ds(pl.multiple_of(h // 8 * 128, 128), 128)], q)
+            buf[:count] = s
+            highest.append(jnp.max(s, axis=0, keepdims=True))
+        return tuple(highest)
+
+    def weigh(bufs, highest, u, low, count, keep):
+        for k, buf in enumerate(bufs):
+            h = u % 8 * 2 + k
+            weights = jnp.exp2(buf[:count] - highest[k])
+            total = jnp.sum(weights, axis=0, keepdims=True)
+            v = vta[pl.ds(pl.multiple_of(h * WIDTH, WIDTH), WIDTH), low : low + count]
+            keep(h, u, dot(v, weights.astype(bf16)), total, highest[k])
+
+    def store(h, u, o, total, highest):
+        att[pl.ds(pl.multiple_of(h * WIDTH, WIDTH), WIDTH), queries_of(u)] = (o * (1.0 / total)).astype(bf16)
+
+    def store_part(h, u, o, total, highest):
+        part_o[h] = o
+        part_l[h] = jnp.broadcast_to(total, (8, QUERIES))
+        part_m[h] = jnp.broadcast_to(highest, (8, QUERIES))
+
+    def store_merged(h, u, o, total, highest):
+        before = part_m[h][:1]
+        top = jnp.maximum(before, highest)
+        was, new = jnp.exp2(before - top), jnp.exp2(highest - top)
+        store(h, u, part_o[h] * was + o * new, part_l[h][:1] * was + total * new, top)
+
+    def two_units(u, highest, span, keep, then):
+        second = scores(odd, u + 1, *span)
+        weigh(even, highest, u, *span, keep)
+        third = then()
+        weigh(odd, second, u + 1, *span, keep)
+        return third
+
+    def sweep(first, count, highest, span, keep, ends=False):
+        def step(i, highest):
+            u = first + 2 * i
+            return two_units(u, highest, span, keep, lambda: scores(even, u + 2, *span))
+
+        highest = lax.fori_loop(0, count // 2 - (1 if ends else 0), step, highest)
+        if ends:
+            two_units(first + count - 2, highest, span, keep, lambda: None)
+        return highest
+
+    def back(block_ids, pages):
+        for k in block_ids:
+            p, m = place(OFFSETS[k])
+            if pages is None:
+                src, dst, at = out2.at[k], in2.at[me], 0
+            else:
+                src, dst, at = out2.at[k, pages], in2.at[me, pages], 1 + pages
+            pltpu.make_async_remote_copy(
+                src_ref=src, dst_ref=dst, send_sem=send2.at[at], recv_sem=recv2.at[at],
+                device_id=(p, m), device_id_type=MESH,
+            ).start()
+
+    def back_half(half):
+        rows = jnp.transpose(att[half * 128 : (half + 1) * 128])
+        out2[FIRST:, half] = dot(comp_t[QUERIES:], rows).reshape(DEVS - FIRST, CAP, 128).astype(bf16)
+        pltpu.make_async_copy(out2.at[DEVS - 1, half], in2.at[me, half], loc2.at[half]).start()
+        back(range(FIRST, DEVS - 1), half)
+
+    mine, other, whole = (0, ROWS), (ROWS, ROWS), (0, 2 * ROWS)
+    sweep(0, 4, scores(even, 0, *mine), mine, store_part, ends=True)
     swap.wait()
     project(1, nrm[1])
-
-    def scores(buf, h):
-        q = qtm[pl.ds(pl.multiple_of(h * 128, 128), 128)]
-        s = dot(keys[:, pl.ds(pl.multiple_of((h // 8) * 128, 128), 128)], q)
-        buf[...] = s
-        return jnp.max(s, axis=0, keepdims=True)
-
-    def weigh(buf, highest, h):
-        p = jnp.exp2(buf[...] - highest).astype(bf16)
-        o = dot(vta[pl.ds(pl.multiple_of(h * 32, 32), 32)], p)
-        att[pl.ds(pl.multiple_of(h * 16, 16), 16)] = (o[:16] / o[16:17]).astype(bf16)
-
-    def two_heads(i, highest):
-        h = 2 * i
-        second = scores(s_b, h + 1)
-        weigh(s_a, highest, h)
-        third = scores(s_a, jnp.minimum(h + 2, HEADS - 1))
-        weigh(s_b, second, h + 1)
-        return third
-
-    lax.fori_loop(0, HEADS // 2, two_heads, scores(s_a, 0))
-
-    attended = jnp.transpose(att[...])
-    out2[...] = to_blocks(dot(comp_t[...], attended)).astype(bf16)
-    exchange(out2, in2, send2, recv2, loc2)
+    sweep(0, 4, scores(even, 0, *other), other, store_merged, ends=True)
+    highest = sweep(4, 4, scores(even, 4, *whole), whole, store)
+    rows = jnp.transpose(att[:, :QUERIES])
+    slots = dot(comp_t[:QUERIES, :QUERIES], rows)
+    for half in range(2):
+        out2[:FIRST, half] = slots[:, half * 128 : (half + 1) * 128].reshape(FIRST, CAP, 128).astype(bf16)
+    back(range(FIRST), None)
+    highest = sweep(8, 4, highest, whole, store)
+    back_half(0)
+    sweep(12, 4, highest, whole, store, ends=True)
+    back_half(1)
+
+    def returned(half):
+        pltpu.make_async_copy(out2.at[0, half], in2.at[0, half], loc2.at[half]).wait()
+        came = in2.at[pl.ds(0, DEVS - 1 - FIRST), half]
+        pltpu.make_async_copy(came, came, recv2.at[1 + half]).wait()
+        return dot(bkt_t[...], in2[:, half].astype(f32).reshape(SLOTS, 128).astype(bf16)).astype(bf16)
 
     own_row = par_ref[...] - me * POOL
     member = onehot(iota((POOL, ROWS), 0) == own_row)
@@ -241,10 +298,12 @@
     for k in range(2):
         e_out[k, :, C:] = edge_counts[8 * k : 8 * k + 8]
 
-    finish(out2, in2, send2, recv2, loc2)
-
-    attended = dot(bkt_t[...], from_blocks(in2[...]).astype(bf16)).astype(bf16)
-    encoded = (pt_ref[...].astype(f32) + dot(attended, wout_ref[...])).astype(bf16)
+    came = in2.at[pl.ds(0, FIRST)]
+    pltpu.make_async_copy(came, came, recv2.at[0]).wait()
+    mixed = pt_ref[...].astype(f32)
+    for half in range(2):
+        mixed = mixed + dot(returned(half), wout_ref[half * 128 : (half + 1) * 128])
+    encoded = mixed.astype(bf16)
     edge_sums = dot(edge_member, encoded)
     for k in range(2):
         e_out[k, :, :C] = edge_sums[8 * k : 8 * k + 8]
@@ -281,6 +340,14 @@
     both = lambda v: jnp.concatenate([v, v], axis=1)
     picked = both(last_cols) * shared_lifted[:1] + both(spilled_cols) * shared_lifted[8:9]
     dec_ref[...] = (partial + picked).astype(bf16)
+
+    most = out1.at[pl.ds(0, (DEVS - 1) * BLK)]
+    pltpu.make_async_copy(most, most, send1).wait()
+    most = out2.at[:FIRST]
+    pltpu.make_async_copy(most, most, send2.at[0]).wait()
+    for half in range(2):
+        most = out2.at[FIRST : DEVS - 1, half]
+        pltpu.make_async_copy(most, most, send2.at[1 + half]).wait()
 
 
 def hand_out(pooled_ref, dec_ref, pooled_out, dec_out, sems):
@@ -313,32 +380,38 @@
             pltpu.VMEM((C, C), bf16),
             pltpu.VMEM((DEVS * BLK, 128), bf16),
             pltpu.VMEM((DEVS * BLK, 128), bf16),
-            pltpu.VMEM((DEVS * BLK, 128), bf16),
-            pltpu.VMEM((DEVS * BLK, 128), bf16),
+            pltpu.VMEM((DEVS, 2, CAP, 128), bf16),
+            pltpu.VMEM((DEVS, 2, CAP, 128), bf16),
             pltpu.VMEM((ROWS, SLOTS), bf16),
             pltpu.VMEM((SLOTS, ROWS), bf16),
             pltpu.VMEM((C, C), bf16),
             pltpu.VMEM((C, C), bf16),
             pltpu.VMEM((2, ROWS, C), bf16),
             pltpu.VMEM((HEADS * 128, ROWS), bf16),
-            pltpu.VMEM((HEADS * 32, 2 * ROWS), bf16),
+            pltpu.VMEM((C, 2 * ROWS), bf16),
             pltpu.VMEM((2 * ROWS, C), bf16),
-            pltpu.VMEM((2 * ROWS, ROWS), f32),
-            pltpu.VMEM((2 * ROWS, ROWS), f32),
+            pltpu.VMEM((2 * ROWS, QUERIES), f32),
+            pltpu.VMEM((2 * ROWS, QUERIES), f32),
+            pltpu.VMEM((2 * ROWS, QUERIES), f32),
+            pltpu.VMEM((2 * ROWS, QUERIES), f32),
             pltpu.VMEM((C, ROWS), bf16),
+            pltpu.VMEM((HEADS // 2, WIDTH, QUERIES), f32),
+            pltpu.VMEM((HEADS // 2, 8, QUERIES), f32),
+            pltpu.VMEM((HEADS // 2, 8, QUERIES), f32),
             pltpu.VMEM((2, 8, C + 128), f32),
             pltpu.VMEM((2, 8, C + 128), f32),
-            dma, dma, dma, dma, dma, dma, dma, dma, dma((2,)), dma((2,)), dma((8,)),
+            dma, dma, dma, dma((3,)), dma((3,)), dma((2,)), dma, dma, dma((2,)), dma((2,)), dma((8,)),
         ],
         compiler_params=pltpu.CompilerParams(
             collective_id=0, has_side_effects=True, vmem_limit_bytes=48 * 1024 * 1024
         ),
     )(*held)
+    results = [pltpu.with_memory_space_constraint(v, pltpu.VMEM) for v in results]
     anywhere = pl.BlockSpec(memory_space=pl.ANY)
     return pl.pallas_call(
         hand_out,
         out_shape=(jax.ShapeDtypeStruct((POOL, C2), bf16), jax.ShapeDtypeStruct((ROWS, C), bf16)),
-        in_specs=[anywhere, anywhere],
+        in_specs=[vmem, vmem],
         out_specs=(anywhere, anywhere),
         scratch_shapes=[dma((2,))],
     )(*results)

time: 67.4 us -> 45 us (0.67)
  Pallas kernels: 65.1 us -> 44.1 us
  local copies, waits for them, and re-layouts: 1.39 us -> 0 us
    pallas_call x1, Pallas kernels: 17 us -> 0.81 us  [on_device(): pl.pallas_call(hand_out, out_shape=(jax.ShapeDtypeStruct((POOL, C2), bf16...]
    pallas_call x1, Pallas kernels: 48.1 us -> 43.3 us  [on_device(): pl.pallas_call(kernel, out_shape=(pltpu.VMEM((POOL, C2), bf16), pltpu.VME...]
    unnamed x4 -> x0, local copies, waits for them, and re-layouts: 1.39 us -> none
where the time goes in v4:
time: 45 us; the launch traced here: 44.9 us
  Pallas kernels  44.1 us (98%)
  between operations  0.8 us (2%)
    pallas_call x1, Pallas kernels, on_device(): pl.pallas_call(kernel, out_shape=(pltpu.VMEM((POOL, C2), bf16), pltpu.VME...  43.3 us

profile of v4, /device:TPU:1, one launch (start us, length us, event | category | flops | bytes accessed | tf_op | source)
XLA Modules:
  0.0 44.9 jit_solution(18246169300722445980)
XLA Ops:
  0.6 43.3 %shard_map.95 = (bf16[256,512]{1,0:T(8,128)(2,1)S(1)}, bf16[512,256]{1,0:T(8,128)(2,1)S(1)}) custom-call(bf16[512,256]{1,0:T(8,128)(2,1)} %refs_0_.1, s32[1,512]{1,0:T(1,128)} %bitcast.2, s32[1,512]{1,0:T(1,128)} %bitcast.3, bf16[256,768]{1,0:T(8,128)(2,1)} %refs_3_.1, bf16[256,256]{1,0:T(8,128)(2,1)} %refs_4_.1, bf16[256,512]{1,0:T(8,128)(2,1)} %refs_5_.1, ...), custom_call_target="tpu_custom_call" | custom-call | tf_op jit(solution)/shard_map/pallas_call | solution.py:367
  43.9 0.8 %shard_map.96 = (bf16[256,512]{1,0:T(8,128)(2,1)}, bf16[512,256]{1,0:T(8,128)(2,1)}) custom-call(bf16[256,512]{1,0:T(8,128)(2,1)S(1)} %get-tuple-element.4.pooled_ref, bf16[512,256]{1,0:T(8,128)(2,1)S(1)} %get-tuple-element.5.dec_ref), custom_call_target="tpu_custom_call" | custom-call | tf_op jit(solution)/shard_map/pallas_call | solution.py:411

commit v5 on v4

--- a/solution.py
+++ b/solution.py
@@ -255,8 +255,8 @@
             ).start()
 
     def back_half(half):
-        rows = jnp.transpose(att[half * 128 : (half + 1) * 128])
-        out2[FIRST:, half] = dot(comp_t[QUERIES:], rows).reshape(DEVS - FIRST, CAP, 128).astype(bf16)
+        slots = dot_nt(comp_t[QUERIES:], att[half * 128 : (half + 1) * 128])
+        out2[FIRST:, half] = slots.reshape(DEVS - FIRST, CAP, 128).astype(bf16)
         pltpu.make_async_copy(out2.at[DEVS - 1, half], in2.at[me, half], loc2.at[half]).start()
         back(range(FIRST, DEVS - 1), half)
 
@@ -266,8 +266,7 @@
     project(1, nrm[1])
     sweep(0, 4, scores(even, 0, *other), other, store_merged, ends=True)
     highest = sweep(4, 4, scores(even, 4, *whole), whole, store)
-    rows = jnp.transpose(att[:, :QUERIES])
-    slots = dot(comp_t[:QUERIES, :QUERIES], rows)
+    slots = dot_nt(comp_t[:QUERIES, :QUERIES], att[:, :QUERIES])
     for half in range(2):
         out2[:FIRST, half] = slots[:, half * 128 : (half + 1) * 128].reshape(FIRST, CAP, 128).astype(bf16)
     back(range(FIRST), None)
@@ -280,7 +279,7 @@
         pltpu.make_async_copy(out2.at[0, half], in2.at[0, half], loc2.at[half]).wait()
         came = in2.at[pl.ds(0, DEVS - 1 - FIRST), half]
         pltpu.make_async_copy(came, came, recv2.at[1 + half]).wait()
-        return dot(bkt_t[...], in2[:, half].astype(f32).reshape(SLOTS, 128).astype(bf16)).astype(bf16)
+        return in2[:, half].astype(f32).reshape(SLOTS, 128).astype(bf16)
 
     own_row = par_ref[...] - me * POOL
     member = onehot(iota((POOL, ROWS), 0) == own_row)
@@ -288,6 +287,8 @@
     counts = jnp.maximum(dot(member, ones), 1.0)
     edge_member = onehot(jnp.where(iota((16, ROWS), 0) < 8, -1, POOL - 1) == own_row)
     edge_counts = dot(edge_member, ones)
+    edge_slots = dot(edge_member, bkt_t[...]).astype(bf16)
+    edge_sums = dot(edge_member, pt_ref[...])
     own_cols = jnp.transpose(jnp.broadcast_to(own_row.astype(f32), (128, ROWS)))
     inner_t = jnp.concatenate(
         [onehot(jnp.where(own_cols == POOL - 1.0, -1.0, own_cols) == lanes + k * 128.0) for k in range(POOL // 128)],
@@ -300,11 +301,14 @@
 
     came = in2.at[pl.ds(0, FIRST)]
     pltpu.make_async_copy(came, came, recv2.at[0]).wait()
-    mixed = pt_ref[...].astype(f32)
+    slots = []
     for half in range(2):
-        mixed = mixed + dot(returned(half), wout_ref[half * 128 : (half + 1) * 128])
-    encoded = mixed.astype(bf16)
-    edge_sums = dot(edge_member, encoded)
+        slots.append(returned(half))
+        sums = dot(edge_slots, slots[half])
+        high = sums.astype(bf16)
+        both_parts = jnp.concatenate([high, (sums - high.astype(f32)).astype(bf16)], axis=0)
+        parts = dot(both_parts, wout_ref[half * 128 : (half + 1) * 128])
+        edge_sums = edge_sums + parts[:16] + parts[16:]
     for k in range(2):
         e_out[k, :, :C] = edge_sums[8 * k : 8 * k + 8]
 
@@ -316,8 +320,28 @@
 
     to_previous = edge(0, (me + DEVS - 1) % DEVS)
     to_next = edge(1, (me + 1) % DEVS)
-    to_previous.start()
-    to_next.start()
+
+    @pl.when(me > 0)
+    def _():
+        to_previous.start()
+
+    @pl.when(me == 0)
+    def _():
+        e_in[1] = jnp.zeros((8, C + 128), f32)
+
+    @pl.when(me < DEVS - 1)
+    def _():
+        to_next.start()
+
+    @pl.when(me == DEVS - 1)
+    def _():
+        e_in[0] = jnp.zeros((8, C + 128), f32)
+
+    mixed = pt_ref[...].astype(f32)
+    for half in range(2):
+        attended = dot(bkt_t[...], slots[half]).astype(bf16)
+        mixed = mixed + dot(attended, wout_ref[half * 128 : (half + 1) * 128])
+    encoded = mixed.astype(bf16)
 
     def pool(sums, tallies):
         mean = sums / jnp.concatenate([tallies, tallies], axis=1)
@@ -331,8 +355,16 @@
     skipped = gelu(layer_norm(dot(encoded, wskip_ref[...])))
     partial = skipped + dot(inner_t, lift(pooled))
 
-    to_previous.wait()
-    to_next.wait()
+    @pl.when(me > 0)
+    def _():
+        to_previous.wait_send()
+        to_next.wait_recv()
+
+    @pl.when(me < DEVS - 1)
+    def _():
+        to_next.wait_send()
+        to_previous.wait_recv()
+
     shared = jnp.concatenate([e_out[1] + e_in[0], e_in[1] + e_out[0]], axis=0)
     shared_pooled = pool(shared[:, :C], jnp.maximum(shared[:, C:], 1.0))
     pooled_ref[POOL - 16 :] = jnp.where(iota((16, C2), 0) == 15, shared_pooled[:1], pooled[POOL - 16 :])

time: 45 us -> 43.8 us (0.973)
  Pallas kernels: 44.1 us -> 43.1 us
    pallas_call x1, Pallas kernels: 43.3 us -> 42.3 us  [on_device(): pl.pallas_call(kernel, out_shape=(pltpu.VMEM((POOL, C2), bf16), pltpu.VME...]
where the time goes in v5:
time: 43.8 us; the launch traced here: 43.7 us
  Pallas kernels  43.1 us (98%)
  between operations  0.64 us (1%)
    pallas_call x1, Pallas kernels, on_device(): pl.pallas_call(kernel, out_shape=(pltpu.VMEM((POOL, C2), bf16), pltpu.VME...  42.3 us

profile of v5, /device:TPU:1, one launch (start us, length us, event | category | flops | bytes accessed | tf_op | source)
XLA Modules:
  0.0 43.7 jit_solution(1504417012715402337)
XLA Ops:
  0.6 42.3 %shard_map.95 = (bf16[256,512]{1,0:T(8,128)(2,1)S(1)}, bf16[512,256]{1,0:T(8,128)(2,1)S(1)}) custom-call(bf16[512,256]{1,0:T(8,128)(2,1)} %refs_0_.1, s32[1,512]{1,0:T(1,128)} %bitcast.2, s32[1,512]{1,0:T(1,128)} %bitcast.3, bf16[256,768]{1,0:T(8,128)(2,1)} %refs_3_.1, bf16[256,256]{1,0:T(8,128)(2,1)} %refs_4_.1, bf16[256,512]{1,0:T(8,128)(2,1)} %refs_5_.1, ...), custom_call_target="tpu_custom_call" | custom-call | tf_op jit(solution)/shard_map/pallas_call | solution.py:399
  42.9 0.8 %shard_map.96 = (bf16[256,512]{1,0:T(8,128)(2,1)}, bf16[512,256]{1,0:T(8,128)(2,1)}) custom-call(bf16[256,512]{1,0:T(8,128)(2,1)S(1)} %get-tuple-element.4.pooled_ref, bf16[512,256]{1,0:T(8,128)(2,1)S(1)} %get-tuple-element.5.dec_ref), custom_call_target="tpu_custom_call" | custom-call | tf_op jit(solution)/shard_map/pallas_call | solution.py:443

commit v6 on v5

--- a/solution.py
+++ b/solution.py
@@ -26,7 +26,8 @@
 def _offsets():
     far = lambda d: min(d, 4 - d)
     every = [(x, y, c, z) for x in range(4) for y in range(4) for z in range(4) for c in range(2)]
-    every.sort(key=lambda o: -(far(o[0]) + far(o[1]) + far(o[3]) + 0.1 * o[2]))
+    mixed = lambda o: (o[0] * 7 + o[1] * 5 + o[3] * 3 + o[2] * 11) % 13
+    every.sort(key=lambda o: -(far(o[0]) + far(o[1]) + far(o[3]) + 0.01 * mixed(o)))
     return [o for o in every if any(o)]
 
 
@@ -232,15 +233,15 @@
         weigh(odd, second, u + 1, *span, keep)
         return third
 
-    def sweep(first, count, highest, span, keep, ends=False):
+    def sweep(first, count, highest, span, keep, then=None):
         def step(i, highest):
             u = first + 2 * i
             return two_units(u, highest, span, keep, lambda: scores(even, u + 2, *span))
 
-        highest = lax.fori_loop(0, count // 2 - (1 if ends else 0), step, highest)
-        if ends:
-            two_units(first + count - 2, highest, span, keep, lambda: None)
-        return highest
+        if then is None:
+            return lax.fori_loop(0, count // 2, step, highest)
+        highest = lax.fori_loop(0, count // 2 - 1, step, highest)
+        return two_units(first + count - 2, highest, span, keep, then)
 
     def back(block_ids, pages):
         for k in block_ids:
@@ -261,18 +262,22 @@
         back(range(FIRST, DEVS - 1), half)
 
     mine, other, whole = (0, ROWS), (ROWS, ROWS), (0, 2 * ROWS)
-    sweep(0, 4, scores(even, 0, *mine), mine, store_part, ends=True)
-    swap.wait()
-    project(1, nrm[1])
-    sweep(0, 4, scores(even, 0, *other), other, store_merged, ends=True)
-    highest = sweep(4, 4, scores(even, 4, *whole), whole, store)
+    def partner():
+        swap.wait()
+        project(1, nrm[1])
+        return scores(even, 0, *other)
+
+    sweep(0, 4, scores(even, 0, *mine), mine, store_part, lambda: None)
+    highest = partner()
+    highest = sweep(0, 4, highest, other, store_merged, lambda: scores(even, 4, *whole))
+    highest = sweep(4, 4, highest, whole, store)
     slots = dot_nt(comp_t[:QUERIES, :QUERIES], att[:, :QUERIES])
     for half in range(2):
         out2[:FIRST, half] = slots[:, half * 128 : (half + 1) * 128].reshape(FIRST, CAP, 128).astype(bf16)
     back(range(FIRST), None)
     highest = sweep(8, 4, highest, whole, store)
     back_half(0)
-    sweep(12, 4, highest, whole, store, ends=True)
+    sweep(12, 4, highest, whole, store, lambda: None)
     back_half(1)
 
     def returned(half):

time: 43.8 us -> 43.1 us (0.984)
  Pallas kernels: 43.1 us -> 42.3 us
    pallas_call x1, Pallas kernels: 42.3 us -> 41.5 us  [on_device(): pl.pallas_call(kernel, out_shape=(pltpu.VMEM((POOL, C2), bf16), pltpu.VME...]
where the time goes in v6:
time: 43.1 us; the launch traced here: 43 us
  Pallas kernels  42.3 us (98%)
  between operations  0.64 us (1%)
    pallas_call x1, Pallas kernels, on_device(): pl.pallas_call(kernel, out_shape=(pltpu.VMEM((POOL, C2), bf16), pltpu.VME...  41.5 us

profile of v6, /device:TPU:1, one launch (start us, length us, event | category | flops | bytes accessed | tf_op | source)
XLA Modules:
  0.0 43.0 jit_solution(16351959068684471938)
XLA Ops:
  0.6 41.5 %shard_map.95 = (bf16[256,512]{1,0:T(8,128)(2,1)S(1)}, bf16[512,256]{1,0:T(8,128)(2,1)S(1)}) custom-call(bf16[512,256]{1,0:T(8,128)(2,1)} %refs_0_.1, s32[1,512]{1,0:T(1,128)} %bitcast.2, s32[1,512]{1,0:T(1,128)} %bitcast.3, bf16[256,768]{1,0:T(8,128)(2,1)} %refs_3_.1, bf16[256,256]{1,0:T(8,128)(2,1)} %refs_4_.1, bf16[256,512]{1,0:T(8,128)(2,1)} %refs_5_.1, ...), custom_call_target="tpu_custom_call" | custom-call | tf_op jit(solution)/shard_map/pallas_call | solution.py:404
  42.2 0.8 %shard_map.96 = (bf16[256,512]{1,0:T(8,128)(2,1)}, bf16[512,256]{1,0:T(8,128)(2,1)}) custom-call(bf16[256,512]{1,0:T(8,128)(2,1)S(1)} %get-tuple-element.4.pooled_ref, bf16[512,256]{1,0:T(8,128)(2,1)S(1)} %get-tuple-element.5.dec_ref), custom_call_target="tpu_custom_call" | custom-call | tf_op jit(solution)/shard_map/pallas_call | solution.py:448
